TPU v7x, 256 devices: a whole 4x4x8 slice. The times are simulated.
256 devices in a mesh: seq: 64 (over z, x, core), head: 4 (over y).
Axes of the slice: x: 4, y: 4, z: 8, core: 2. Of those that a mesh axis runs over, the one named last changes fastest.
Arguments:
- query: bfloat16 [16384, 2048], P('seq', 'head'), may hold values from -24 to 24
- key: bfloat16 [16384, 512], P('seq', 'head'), may hold values from -24 to 24
- value: bfloat16 [16384, 512], P('seq', 'head'), may hold values from -6 to 6
- grad_out: bfloat16 [16384, 2048], P('seq', 'head'), may hold values from -6 to 6
- gate_score: int32 [4, 32, 32], P('head'), may hold values from 0 to 1048575
Outputs:
- attended: bfloat16 [16384, 2048], P('seq', 'head')
- grad_query: bfloat16 [16384, 2048], P('seq', 'head')
- grad_key: bfloat16 [16384, 512], P('seq', 'head')
- grad_value: bfloat16 [16384, 512], P('seq', 'head')
All inputs are finite; a program needn't handle non-finite values.
Results may differ from a plain program's by a relative error of at most 0.03.
Values may be sent and summed in bfloat16 or wider, within the bound.
No kernel may reach another device: no remote copies, remote signals or barrier semaphores. Data moves between devices by JAX's collectives and lax.ppermute only.
A program may use at most 192 MiB of HBM per device.

v0:
```python
import functools
import math

import jax
import jax.numpy as jnp
from jax import lax
from jax.experimental import pallas as pl
from jax.experimental.pallas import tpu as pltpu
from jax.sharding import Mesh
from jax.sharding import PartitionSpec as P

HEAD_DIM = 128
GROUP = 4
TOPK = 8
NBLK = 32
HALF = 256
COLS = GROUP * HALF
SCALE = 1.0 / math.sqrt(HEAD_DIM)
SCALE2 = SCALE / math.log(2.0)
NEG = -1e30
MASKED = -3e38
BF = jnp.bfloat16
F32 = jnp.float32
SIZES = {"z": 8, "x": 4, "core": 2, "head": 4}
NT = (((1,), (1,)), ((), ()))
NN = (((1,), (0,)), ((), ()))
CORE_AT = 32
VMEM_LIMIT = 40 * 1024 * 1024
STAT = (2, 3, COLS)
ACC = (HEAD_DIM, COLS)
ROWS = (COLS, HEAD_DIM)
PIECE = (HALF, 2 * HEAD_DIM)
SLOT_FLOPS = 2 * HALF * 2 * COLS * HEAD_DIM


def dot(a, b, dims):
    return lax.dot_general(a, b, dims, preferred_element_type=F32)


def wide(a):
    return a.astype(F32)


def shift(a, axis, d):
    n = SIZES[axis]
    return lax.ppermute(a, axis, [(i, (i + d) % n) for i in range(n)])


def keep_mask(off):
    i = lax.broadcasted_iota(jnp.int32, (HALF, HALF), 0)
    j = lax.broadcasted_iota(jnp.int32, (HALF, HALF), 1)
    return (i - j) <= off


def fetch(i, kv_refs, sizes, kv_buf):
    if len(kv_refs) == 1:
        return kv_refs[0][0]

    @pl.when(i < sizes[0])
    def _():
        kv_buf[...] = kv_refs[0][0]

    @pl.when(i >= sizes[0])
    def _():
        kv_buf[...] = kv_refs[1][0]

    return kv_buf[...]


def forward_kernel(base, sizes, first, last, info, *refs):
    n = len(sizes)
    kv_refs, refs = refs[:n], refs[n:]
    q_refs, refs = refs[:2], refs[2:]
    if last:
        g_refs, refs = refs[:2], refs[2:]
    if not first:
        stat_in, acc_in, refs = refs[0], refs[1:3], refs[3:]
    stat_ref, acc_refs, (s_ref, p_ref, kv_buf) = refs[0], refs[1:3], refs[3:]
    i = pl.program_id(0)
    core = info[CORE_AT]

    @pl.when(i == 0)
    def _():
        if first:
            stat_ref[:, 0:1, :] = jnp.full((2, 1, COLS), NEG, F32)
            stat_ref[:, 1:3, :] = jnp.zeros((2, 2, COLS), F32)
            for half in range(2):
                acc_refs[half][...] = jnp.zeros(ACC, F32)
        else:
            stat_ref[...] = stat_in[...]
            for half in range(2):
                acc_refs[half][...] = acc_in[half][...]

    def step(masked):
        kv = fetch(i, kv_refs, sizes, kv_buf)
        k = kv[:, :HEAD_DIM]
        vt = jnp.transpose(kv[:, HEAD_DIM:])
        for half in range(2):
            s_ref[:, pl.ds(half * COLS, COLS)] = dot(k, q_refs[half][...], NT)
        for half in range(2):
            acc = acc_refs[half]
            if masked:
                keep = keep_mask(half * HALF * (1 - 2 * core))
            for h in range(GROUP):
                cols = pl.ds(h * HALF, HALF)
                flat = pl.ds(half * COLS + h * HALF, HALF)
                s = s_ref[:, flat]
                if masked:
                    s = jnp.where(keep, s, MASKED)
                m_old = stat_ref[half, 0:1, cols]
                m_new = jnp.maximum(m_old, jnp.max(s, axis=0, keepdims=True) * SCALE2)
                alpha = jnp.exp2(m_old - m_new)
                p = jnp.exp2(s * SCALE2 - m_new)
                stat_ref[half, 0:1, cols] = m_new
                stat_ref[half, 1:2, cols] = stat_ref[half, 1:2, cols] * alpha + jnp.sum(p, axis=0, keepdims=True)
                acc[:, cols] = acc[:, cols] * alpha
                p_ref[:, flat] = p.astype(BF)
            acc[...] += dot(vt, p_ref[:, pl.ds(half * COLS, COLS)], NN)

    if first:
        pl.when(i == 0)(lambda: step(True))
        pl.when((i > 0) & (info[base + i] > 0))(lambda: step(False))
    else:
        pl.when(info[base + i] > 0)(lambda: step(False))

    if last:

        @pl.when(i == sum(sizes) - 1)
        def _():
            eye = (
                lax.broadcasted_iota(jnp.int32, (HEAD_DIM, HEAD_DIM), 0)
                == lax.broadcasted_iota(jnp.int32, (HEAD_DIM, HEAD_DIM), 1)
            ).astype(F32).astype(BF)
            for half in range(2):
                turned = dot(eye, g_refs[half][...], NT)
                stat_ref[half, 2:3, :] = jnp.sum(turned * acc_refs[half][...], axis=0, keepdims=True)


def combine(mine, other, half):
    m0 = mine[half, 0:1, :]
    m1 = other[1 - half, 0:1, :]
    m = jnp.maximum(m0, m1)
    e0 = jnp.exp2(m0 - m)
    e1 = jnp.exp2(m1 - m)
    total = mine[half, 1:2, :] * e0 + other[1 - half, 1:2, :] * e1
    return m + jnp.log2(total), e0 / total, e1 / total


def backward_kernel(base, sizes, first, masks, info, *refs):
    n = len(sizes)
    kv_refs, refs = refs[:n], refs[n:]
    q_refs, g_refs, mine, other, refs = refs[:2], refs[2:4], refs[4], refs[5], refs[6:]
    if not first:
        dq_in, refs = refs[:2], refs[2:]
    dq_refs, out_refs, refs = refs[:2], refs[2 : 2 + n], refs[2 + n :]
    row_ref, s_ref, dp_ref, p_ref, ds_ref, kv_buf, out_buf = refs
    i = pl.program_id(0)
    core = info[CORE_AT]

    @pl.when(i == 0)
    def _():
        for half in range(2):
            lse, w0, w1 = combine(mine, other, half)
            row_ref[half, 0:1, :] = lse
            row_ref[half, 1:2, :] = mine[half, 2:3, :] * w0 + other[1 - half, 2:3, :] * w1
            dq_refs[half][...] = jnp.zeros(ACC, F32) if first else dq_in[half][...]

    def step(masked):
        kv = fetch(i, kv_refs, sizes, kv_buf)
        k = kv[:, :HEAD_DIM]
        v = kv[:, HEAD_DIM:]
        kt = jnp.transpose(k)
        for half in range(2):
            cols = pl.ds(half * COLS, COLS)
            s_ref[:, cols] = dot(k, q_refs[half][...], NT)
            dp_ref[:, cols] = dot(v, g_refs[half][...], NT)
        for half in range(2):
            if masked:
                keep = keep_mask(half * HALF * (1 - 2 * core))
            for h in range(GROUP):
                cols = pl.ds(h * HALF, HALF)
                flat = pl.ds(half * COLS + h * HALF, HALF)
                p = jnp.exp2(s_ref[:, flat] * SCALE2 - row_ref[half, 0:1, cols])
                if masked:
                    p = jnp.where(keep, p, 0.0)
                p_ref[:, flat] = p.astype(BF)
                ds_ref[:, flat] = (p * (dp_ref[:, flat] - row_ref[half, 1:2, cols])).astype(BF)
            dq_refs[half][...] += dot(kt, ds_ref[:, pl.ds(half * COLS, COLS)], NN)
        dk = jnp.zeros((HALF, HEAD_DIM), F32)
        dv = jnp.zeros((HALF, HEAD_DIM), F32)
        for half in range(2):
            cols = pl.ds(half * COLS, COLS)
            dk = dk + dot(ds_ref[:, cols], q_refs[half][...], NN)
            dv = dv + dot(p_ref[:, cols], g_refs[half][...], NN)
        out_buf[:, :HEAD_DIM] = dk.astype(BF)
        out_buf[:, HEAD_DIM:] = dv.astype(BF)

    live = info[base + i] > 0
    if masks:
        pl.when(i == 0)(lambda: step(True))
        pl.when((i > 0) & live)(lambda: step(False))
    else:
        pl.when(live)(lambda: step(False))

    @pl.when(jnp.logical_not(live))
    def _():
        out_buf[...] = jnp.zeros(PIECE, BF)

    if n == 1:
        out_refs[0][0] = out_buf[...]
    else:

        @pl.when(i < sizes[0])
        def _():
            out_refs[0][0] = out_buf[...]

        @pl.when(i >= sizes[0])
        def _():
            out_refs[1][0] = out_buf[...]


def finish_kernel(mine, other, acc_mine, acc_other, dq_mine, dq_other, att_ref, dq_ref):
    lse, w0, w1 = combine(mine, other, 0)
    for h in range(GROUP):
        cols = slice(h * HALF, (h + 1) * HALF)
        rows = slice(h * HEAD_DIM, (h + 1) * HEAD_DIM)
        out = acc_mine[:, cols] * w0[:, cols] + acc_other[:, cols] * w1[:, cols]
        att_ref[:, rows] = jnp.transpose(out).astype(BF)
        dq_ref[:, rows] = jnp.transpose((dq_mine[:, cols] + dq_other[:, cols]) * SCALE).astype(BF)


def whole(shape):
    return pl.BlockSpec(shape, lambda i, info: (0,) * len(shape))


def piece_specs(sizes):
    block = (1,) + PIECE
    if len(sizes) == 1:
        return [pl.BlockSpec(block, lambda i, info: (i, 0, 0))]
    n = sizes[0]
    return [
        pl.BlockSpec(block, lambda i, info: (jnp.minimum(i, n - 1), 0, 0)),
        pl.BlockSpec(block, lambda i, info: (jnp.maximum(i - n, 0), 0, 0)),
    ]


def cost(slots, products):
    return pl.CostEstimate(
        flops=slots * products * SLOT_FLOPS, bytes_accessed=1 << 22, transcendentals=slots * HALF * 2 * COLS
    )


def forward(base, info, kvs, q, state, g):
    sizes = [a.shape[0] for a in kvs]
    first = state is None
    last = g is not None
    ins = list(kvs) + list(q) + (list(g) if last else []) + ([] if first else list(state))
    specs = piece_specs(sizes) + [whole(ROWS)] * (4 if last else 2)
    if not first:
        specs += [whole(STAT), whole(ACC), whole(ACC)]
    return pl.pallas_call(
        functools.partial(forward_kernel, base, sizes, first, last),
        grid_spec=pltpu.PrefetchScalarGridSpec(
            num_scalar_prefetch=1,
            grid=(sum(sizes),),
            in_specs=specs,
            out_specs=[whole(STAT), whole(ACC), whole(ACC)],
            scratch_shapes=[
                pltpu.VMEM((HALF, 2 * COLS), F32),
                pltpu.VMEM((HALF, 2 * COLS), BF),
                pltpu.VMEM(PIECE, BF),
            ],
        ),
        out_shape=[jax.ShapeDtypeStruct(s, F32) for s in (STAT, ACC, ACC)],
        compiler_params=pltpu.CompilerParams(vmem_limit_bytes=VMEM_LIMIT),
        cost_estimate=cost(3, 2),
        name="forward",
    )(info, *ins)


def backward(base, info, kvs, q, g, mine, other, dq):
    sizes = [a.shape[0] for a in kvs]
    first = dq is None
    ins = list(kvs) + list(q) + list(g) + [mine, other] + ([] if first else list(dq))
    specs = piece_specs(sizes) + [whole(ROWS)] * 4 + [whole(STAT)] * 2
    if not first:
        specs += [whole(ACC), whole(ACC)]
    wide_shape = (HALF, 2 * COLS)
    res = pl.pallas_call(
        functools.partial(backward_kernel, base, sizes, first, base == 0),
        grid_spec=pltpu.PrefetchScalarGridSpec(
            num_scalar_prefetch=1,
            grid=(sum(sizes),),
            in_specs=specs,
            out_specs=[whole(ACC), whole(ACC)] + piece_specs(sizes),
            scratch_shapes=[
                pltpu.VMEM((2, 2, COLS), F32),
                pltpu.VMEM(wide_shape, F32),
                pltpu.VMEM(wide_shape, F32),
                pltpu.VMEM(wide_shape, BF),
                pltpu.VMEM(wide_shape, BF),
                pltpu.VMEM(PIECE, BF),
                pltpu.VMEM(PIECE, BF),
            ],
        ),
        out_shape=[jax.ShapeDtypeStruct(ACC, F32)] * 2 + [jax.ShapeDtypeStruct(a.shape, BF) for a in kvs],
        compiler_params=pltpu.CompilerParams(vmem_limit_bytes=VMEM_LIMIT),
        cost_estimate=cost(3, 5),
        name="backward",
    )(info, *ins)
    return res[:2], res[2:]


def finish(mine, other, acc_mine, acc_other, dq_mine, dq_other):
    shape = jax.ShapeDtypeStruct((HALF, GROUP * HEAD_DIM), BF)
    return pl.pallas_call(
        finish_kernel,
        out_shape=[shape, shape],
        compiler_params=pltpu.CompilerParams(vmem_limit_bytes=VMEM_LIMIT),
        cost_estimate=pl.CostEstimate(flops=1 << 20, bytes_accessed=1 << 22, transcendentals=0),
        name="finish",
    )(mine, other, acc_mine, acc_other, dq_mine, dq_other)


def plan(gate_score):
    z = lax.axis_index("z")
    x = lax.axis_index("x")
    own = z * 4 + x
    mine = lax.optimization_barrier(gate_score.reshape(8, 128))
    totals = mine + shift(mine, "head", 1) + shift(mine, "head", 2) + shift(mine, "head", 3)
    row = lax.dynamic_slice_in_dim(totals.reshape(NBLK, NBLK), own, 1, 0)[0]
    columns = jnp.arange(NBLK, dtype=jnp.int32)
    ranked = jnp.where(columns < own, row * NBLK + columns, -1)
    rank = jnp.sum((ranked[None, :] > ranked[:, None]).astype(jnp.int32), axis=1)
    used = ((rank < TOPK) & (ranked >= 0)) | (columns == own)
    dz = (z - columns // 4) % 8
    dx = (x - columns % 4) % 4
    group = jnp.where(dx < 2, dx, 5 - dx)
    place = group * 8 + dz
    live = jnp.sum((place[None, :] == columns[:, None]) & used[None, :], axis=1, dtype=jnp.int32)
    return jnp.concatenate([live, lax.axis_index("core")[None]])


def heads_first(a):
    return jnp.transpose(a.reshape(HALF, GROUP, HEAD_DIM), (1, 0, 2)).reshape(ROWS)


def gather_z(piece):
    a1, b1 = shift(piece, "z", 1), shift(piece, "z", -1)
    a2, b2 = shift(piece, "z", 2), shift(piece, "z", -2)
    a3, b3, a4 = shift(a2, "z", 1), shift(b2, "z", -1), shift(a2, "z", 2)
    return jnp.stack([piece, a1, a2, a3, a4, b3, b2, b1])


def scatter_z(t):
    a = shift(t[3], "z", -1)
    b = shift(t[4], "z", -2)
    c = shift(t[5], "z", 1)
    t2 = (wide(t[2]) + wide(a) + wide(b)).astype(BF)
    t6 = (wide(t[6]) + wide(c)).astype(BF)
    parts = [shift(t2, "z", -2), shift(t[1], "z", -1), shift(t6, "z", 2), shift(t[7], "z", 1)]
    return wide(t[0]) + sum(wide(a) for a in parts)


def on_device(query, key, value, grad_out, gate_score):
    swap = functools.partial(shift, axis="core", d=1)
    kv0 = gather_z(jnp.concatenate([key, value], axis=1))
    q = heads_first(query)
    g = heads_first(grad_out)
    q = (q, swap(q))
    g = (g, swap(g))
    info = plan(gate_score)

    kv1 = shift(kv0, "x", 1)
    kv3 = shift(kv0, "x", -1)
    kv2 = (shift(kv1[:4], "x", 1), shift(kv3[4:], "x", -1))

    state = forward(0, info, [kv0], q, None, None)
    state = forward(8, info, [kv1, kv3], q, state, None)
    mine, acc, acc_away = forward(24, info, kv2, q, state, g)
    other = swap(mine)
    acc_other = swap(acc_away)

    dq, (low, high) = backward(24, info, kv2, q, g, mine, other, None)
    low = shift(low, "x", -1)
    high = shift(high, "x", 1)
    dq, (t1, t3) = backward(8, info, [kv1, kv3], q, g, mine, other, dq)
    t1 = jnp.concatenate([(wide(t1[:4]) + wide(low)).astype(BF), t1[4:]])
    t3 = jnp.concatenate([t3[:4], (wide(t3[4:]) + wide(high)).astype(BF)])
    t1 = shift(t1, "x", -1)
    t3 = shift(t3, "x", 1)
    dq, (t0,) = backward(0, info, [kv0], q, g, mine, other, dq)
    total = scatter_z((wide(t0) + wide(t1) + wide(t3)).astype(BF))
    grad_key = (total[:, :HEAD_DIM] * SCALE).astype(BF)
    grad_value = total[:, HEAD_DIM:].astype(BF)
    attended, grad_query = finish(mine, other, acc, acc_other, dq[0], swap(dq[1]))
    return (attended, grad_query, grad_key, grad_value)


def solution(mesh):
    devices = mesh.devices.reshape(8, 4, 2, 4)
    split = Mesh(devices, ("z", "x", "core", "head"))
    spec = P(("z", "x", "core"), "head")
    return jax.shard_map(
        on_device,
        mesh=split,
        in_specs=(spec, spec, spec, spec, P("head", None, None)),
        out_specs=(spec, spec, spec, spec),
        check_vma=False,
    )
```

profile of v0, /device:TPU:14, one launch (start us, length us, event | category | flops | bytes accessed | tf_op | source)
XLA Modules:
  0.0 162.1 jit_solution(14562015818593670310)
XLA Ops:
  0.6 0.8 reshape.118
  1.5 0.5 collective-permute-start.2
  1.9 2.6 %collective-permute-start.1 = (s32[8,128]{1,0:T(8,128)S(1)}, s32[8,128]{1,0:T(8,128)S(1)}, u32[]{:S(2)}, u32[]{:S(2)}) collective-permute-start(s32[8,128]{1,0:T(8,128)S(1)} %reshape.118), channel_id=1, source_target_pairs={{0,2},{1,3},{2,0},{3,1},{4,6},{5,7},{6,4},{7,5},{8,10},{9,11},{10,... | collective-permute-start | bytes 12296 | tf_op jit(solution)/shard_map/ppermute | solution.py:46
  4.5 1.9 %collective-permute-start = (s32[8,128]{1,0:T(8,128)S(1)}, s32[8,128]{1,0:T(8,128)S(1)}, u32[]{:S(2)}, u32[]{:S(2)}) collective-permute-start(s32[8,128]{1,0:T(8,128)S(1)} %reshape.118), channel_id=1, source_target_pairs={{0,1},{1,2},{2,3},{3,0},{4,5},{5,6},{6,7},{7,4},{8,9},{9,10},{10,1... | collective-permute-start | bytes 12296 | tf_op jit(solution)/shard_map/ppermute | solution.py:46
  6.4 0.9 constant_dynamic-update-slice_fusion.1
  7.3 0.9 constant_dynamic-update-slice_fusion
  8.1 3.3 %collective-permute-start.4 = (bf16[256,256]{1,0:T(8,128)(2,1)S(1)}, bf16[256,256]{1,0:T(8,128)(2,1)S(1)}, u32[]{:S(2)}, u32[]{:S(2)}) collective-permute-start(bf16[256,256]{1,0:T(8,128)(2,1)S(1)} %constant_dynamic-update-slice_fusion), channel_id=1, source_target_pairs={{0,64},{32,96},{64,128},{96,160},{128,192},{160,224},{192,0},{224,... | collective-permute-start | bytes 393224 | tf_op jit(solution)/shard_map/ppermute | solution.py:46
  11.5 1.9 %collective-permute-start.3 = (bf16[256,256]{1,0:T(8,128)(2,1)S(1)}, bf16[256,256]{1,0:T(8,128)(2,1)S(1)}, u32[]{:S(2)}, u32[]{:S(2)}) collective-permute-start(bf16[256,256]{1,0:T(8,128)(2,1)S(1)} %constant_dynamic-update-slice_fusion), channel_id=1, source_target_pairs={{0,32},{32,64},{64,96},{96,128},{128,160},{160,192},{192,224},{224... | collective-permute-start | bytes 393224 | tf_op jit(solution)/shard_map/ppermute | solution.py:46
  13.4 0.6 bitcast_dynamic-update-slice_fusion.7
  14.0 7.2 %collective-permute-done.4 = bf16[256,256]{1,0:T(8,128)(2,1)S(1)} collective-permute-done((bf16[256,256]{1,0:T(8,128)(2,1)S(1)}, bf16[256,256]{1,0:T(8,128)(2,1)S(1)}, u32[]{:S(2)}, u32[]{:S(2)}) %collective-permute-start.4) | collective-permute-done | bytes 131104 | tf_op jit(solution)/shard_map/ppermute | solution.py:46
  21.3 1.9 %collective-permute-start.7 = (bf16[256,256]{1,0:T(8,128)(2,1)S(1)}, bf16[256,256]{1,0:T(8,128)(2,1)S(1)}, u32[]{:S(2)}, u32[]{:S(2)}) collective-permute-start(bf16[256,256]{1,0:T(8,128)(2,1)S(1)} %constant_dynamic-update-slice_fusion), channel_id=1, source_target_pairs={{0,192},{32,224},{64,0},{96,32},{128,64},{160,96},{192,128},{224,1... | collective-permute-start | bytes 393224 | tf_op jit(solution)/shard_map/ppermute | solution.py:46
  23.2 0.5 collective-permute-start.5
  23.7 0.7 bitcast_dynamic-update-slice_fusion.6
  24.4 0.7 bitcast_dynamic-update-slice_fusion.5
  25.1 4.3 %collective-permute-done.5 = bf16[256,256]{1,0:T(8,128)(2,1)S(1)} collective-permute-done((bf16[256,256]{1,0:T(8,128)(2,1)S(1)}, bf16[256,256]{1,0:T(8,128)(2,1)S(1)}, u32[]{:S(2)}, u32[]{:S(2)}) %collective-permute-start.5) | collective-permute-done | bytes 131104 | tf_op jit(solution)/shard_map/ppermute | solution.py:46
  29.4 0.7 bitcast_dynamic-update-slice_fusion.4
  30.0 3.4 %collective-permute-start.9 = (bf16[256,256]{1,0:T(8,128)(2,1)S(1)}, bf16[256,256]{1,0:T(8,128)(2,1)S(1)}, u32[]{:S(2)}, u32[]{:S(2)}) collective-permute-start(bf16[256,256]{1,0:T(8,128)(2,1)S(1)} %constant_dynamic-update-slice_fusion), channel_id=1, source_target_pairs={{0,224},{32,0},{64,32},{96,64},{128,96},{160,128},{192,160},{224,1... | collective-permute-start | bytes 393224 | tf_op jit(solution)/shard_map/ppermute | solution.py:46
  33.5 3.1 %collective-permute-done.6 = bf16[256,256]{1,0:T(8,128)(2,1)S(1)} collective-permute-done((bf16[256,256]{1,0:T(8,128)(2,1)S(1)}, bf16[256,256]{1,0:T(8,128)(2,1)S(1)}, u32[]{:S(2)}, u32[]{:S(2)}) %collective-permute-start.6) | collective-permute-done | bytes 131104 | tf_op jit(solution)/shard_map/ppermute | solution.py:46
  36.6 2.5 %collective-permute-start.8 = (bf16[256,256]{1,0:T(8,128)(2,1)S(1)}, bf16[256,256]{1,0:T(8,128)(2,1)S(1)}, u32[]{:S(2)}, u32[]{:S(2)}) collective-permute-start(bf16[256,256]{1,0:T(8,128)(2,1)S(1)} %collective-permute-done.7), channel_id=1, source_target_pairs={{0,224},{32,0},{64,32},{96,64},{128,96},{160,128},{192,160},{224,1... | collective-permute-start | bytes 393224 | tf_op jit(solution)/shard_map/ppermute | solution.py:46
  39.0 0.7 bitcast_dynamic-update-slice_fusion.3
  39.7 1.9 %collective-permute-done.8 = bf16[256,256]{1,0:T(8,128)(2,1)S(1)} collective-permute-done((bf16[256,256]{1,0:T(8,128)(2,1)S(1)}, bf16[256,256]{1,0:T(8,128)(2,1)S(1)}, u32[]{:S(2)}, u32[]{:S(2)}) %collective-permute-start.8) | collective-permute-done | bytes 131104 | tf_op jit(solution)/shard_map/ppermute | solution.py:46
  41.6 0.6 bitcast_dynamic-update-slice_fusion.2
  42.2 0.7 bitcast_dynamic-update-slice_fusion.1
  42.9 0.7 bitcast_dynamic-update-slice_fusion.refs_0_
  43.5 0.8 collective-permute-start.12
  44.4 2.4 %collective-permute-start.10 = (bf16[8,256,256]{2,1,0:T(8,128)(2,1)}, bf16[8,256,256]{2,1,0:T(8,128)(2,1)S(1)}, u32[]{:S(2)}, u32[]{:S(2)}) collective-permute-start(bf16[8,256,256]{2,1,0:T(8,128)(2,1)} %bitcast_dynamic-update-slice_fusion.refs_0_), channel_id=1, source_target_pairs={{0,8},{8,16},{16,24},{24,0},{1,9},{9,17},{17,25},{25,1},{2,10},{10... | collective-permute-start | bytes 3145736 | tf_op jit(solution)/shard_map/ppermute | solution.py:46
  47.0 0.5 collective-permute-start.14
  47.6 0.2 convert_reduce_fusion.1
  47.8 19.1 %collective-permute-done.12.refs_1_ = bf16[8,256,256]{2,1,0:T(8,128)(2,1)S(1)} collective-permute-done((bf16[8,256,256]{2,1,0:T(8,128)(2,1)}, bf16[8,256,256]{2,1,0:T(8,128)(2,1)S(1)}, u32[]{:S(2)}, u32[]{:S(2)}) %collective-permute-start.12) | collective-permute-done | bytes 1048608 | tf_op jit(solution)/shard_map/ppermute | solution.py:46
  67.0 0.2 collective-permute-start.13
  67.3 3.3 %collective-permute-start.11 = (bf16[4,256,256]{2,1,0:T(8,128)(2,1)S(1)}, bf16[4,256,256]{2,1,0:T(8,128)(2,1)S(1)}, u32[]{:S(2)}, u32[]{:S(2)}) collective-permute-start(bf16[4,256,256]{2,1,0:T(8,128)(2,1)S(1)} %slice.65), channel_id=1, source_target_pairs={{0,8},{8,16},{16,24},{24,0},{1,9},{9,17},{17,25},{25,1},{2,10},{10... | collective-permute-start | bytes 1572872 | tf_op jit(solution)/shard_map/ppermute | solution.py:46
  70.6 0.1 convert_reduce_fusion
  70.8 5.3 %forward.3 = (f32[2,3,1024]{2,1,0:T(4,128)S(1)}, f32[128,1024]{1,0:T(8,128)S(1)}, f32[128,1024]{1,0:T(8,128)S(1)}) custom-call(s32[33]{0:T(128)S(1)} %pad_add_fusion.info, bf16[8,256,256]{2,1,0:T(8,128)(2,1)} %bitcast_dynamic-update-slice_fusion.refs_0_, bf16[1024,128]{1,0:T(8,128)(2,1)S(1)} %bitcast.73, ...), custom_call_target="tpu_custom_call" | custom-call | flops 805306368 | bytes 4194304 | tf_op jit(solution)/shard_map/forward/pallas_call | solution.py:261
  76.2 3.2 %forward.4 = (f32[2,3,1024]{2,1,0:T(4,128)S(1)}, f32[128,1024]{1,0:T(8,128)S(1)}, f32[128,1024]{1,0:T(8,128)S(1)}) custom-call(s32[33]{0:T(128)S(1)} %pad_add_fusion.info, bf16[8,256,256]{2,1,0:T(8,128)(2,1)S(1)} %collective-permute-done.10.refs_0_, bf16[8,256,256]{2,1,0:T(8,128)(2,1)S(1)} %collective-permute-done.12.refs_1_, ...), custom_call_target="tpu_custom_call" | custom-call | flops 805306368 | bytes 4194304 | tf_op jit(solution)/shard_map/forward/pallas_call | solution.py:261
  79.4 2.3 %forward.5 = (f32[2,3,1024]{2,1,0:T(4,128)S(1)}, f32[128,1024]{1,0:T(8,128)S(1)}, f32[128,1024]{1,0:T(8,128)S(1)}) custom-call(s32[33]{0:T(128)S(1)} %pad_add_fusion.info, bf16[4,256,256]{2,1,0:T(8,128)(2,1)S(1)} %collective-permute-done.11.refs_0_, bf16[4,256,256]{2,1,0:T(8,128)(2,1)S(1)} %collective-permute-done.13.refs_1_, ...), custom_call_target="tpu_custom_call" | custom-call | flops 805306368 | bytes 4194304 | tf_op jit(solution)/shard_map/forward/pallas_call | solution.py:261
  81.7 1.2 collective-permute-done.16.refs_7_.refs_6_.other
  82.9 2.6 %backward.3 = (f32[128,1024]{1,0:T(8,128)S(1)}, f32[128,1024]{1,0:T(8,128)S(1)}, bf16[4,256,256]{2,1,0:T(8,128)(2,1)S(1)}, bf16[4,256,256]{2,1,0:T(8,128)(2,1)S(1)}) custom-call(s32[33]{0:T(128)S(1)} %pad_add_fusion.info, bf16[4,256,256]{2,1,0:T(8,128)(2,1)S(1)} %collective-permute-done.11.refs_0_, bf16[4,256,256]{2,1,0:T(8,128)(2,1)S(1)} %collective-permute-done.13.refs_1_, ...), custom_call_target="tpu_custom_call" | custom-call | flops 2013265920 | bytes 4194304 | tf_op jit(solution)/shard_map/backward/pallas_call | solution.py:289
  85.6 2.0 %collective-permute-start.19 = (bf16[4,256,256]{2,1,0:T(8,128)(2,1)S(1)}, bf16[4,256,256]{2,1,0:T(8,128)(2,1)S(1)}, u32[]{:S(2)}, u32[]{:S(2)}) collective-permute-start(bf16[4,256,256]{2,1,0:T(8,128)(2,1)S(1)} %get-tuple-element.45), channel_id=1, source_target_pairs={{0,24},{8,0},{16,8},{24,16},{1,25},{9,1},{17,9},{25,17},{2,26},{10... | collective-permute-start | bytes 1572872 | tf_op jit(solution)/shard_map/ppermute | solution.py:46
  87.6 4.5 %backward.4 = (f32[128,1024]{1,0:T(8,128)S(1)}, f32[128,1024]{1,0:T(8,128)S(1)}, bf16[8,256,256]{2,1,0:T(8,128)(2,1)S(1)}, bf16[8,256,256]{2,1,0:T(8,128)(2,1)S(1)}) custom-call(s32[33]{0:T(128)S(1)} %pad_add_fusion.info, bf16[8,256,256]{2,1,0:T(8,128)(2,1)S(1)} %collective-permute-done.10.refs_0_, bf16[8,256,256]{2,1,0:T(8,128)(2,1)S(1)} %collective-permute-done.12.refs_1_, ...), custom_call_target="tpu_custom_call" | custom-call | flops 2013265920 | bytes 4194304 | tf_op jit(solution)/shard_map/backward/pallas_call | solution.py:289
  92.2 7.4 %collective-permute-done.21 = bf16[4,256,256]{2,1,0:T(8,128)(2,1)S(1)} collective-permute-done((bf16[4,256,256]{2,1,0:T(8,128)(2,1)S(1)}, bf16[4,256,256]{2,1,0:T(8,128)(2,1)S(1)}, u32[]{:S(2)}, u32[]{:S(2)}) %collective-permute-start.21) | collective-permute-done | bytes 524320 | tf_op jit(solution)/shard_map/ppermute | solution.py:46
  99.6 0.1 add_convert_fusion.1
  99.8 1.6 collective-permute-start.22
  101.4 0.1 add_convert_fusion.2
  101.5 0.1 pad_maximum_fusion
  101.6 0.6 collective-permute-start.20
  102.3 6.1 %backward.5 = (f32[128,1024]{1,0:T(8,128)S(1)}, f32[128,1024]{1,0:T(8,128)S(1)}, bf16[8,256,256]{2,1,0:T(8,128)(2,1)S(1)}) custom-call(s32[33]{0:T(128)S(1)} %pad_add_fusion.info, bf16[8,256,256]{2,1,0:T(8,128)(2,1)} %bitcast_dynamic-update-slice_fusion.refs_0_, bf16[1024,128]{1,0:T(8,128)(2,1)S(1)} %bitcast.78, ...), custom_call_target="tpu_custom_call" | custom-call | flops 2013265920 | bytes 4194304 | tf_op jit(solution)/shard_map/backward/pallas_call | solution.py:289
  108.4 0.6 collective-permute-start.18
  109.0 15.3 %collective-permute-done.22 = bf16[8,256,256]{2,1,0:T(8,128)(2,1)S(1)} collective-permute-done((bf16[8,256,256]{2,1,0:T(8,128)(2,1)S(1)}, bf16[8,256,256]{2,1,0:T(8,128)(2,1)S(1)}, u32[]{:S(2)}, u32[]{:S(2)}) %collective-permute-start.22) | collective-permute-done | bytes 1048608 | tf_op jit(solution)/shard_map/ppermute | solution.py:46
  124.3 3.1 %collective-permute-done.20 = bf16[8,256,256]{2,1,0:T(8,128)(2,1)S(1)} collective-permute-done((bf16[8,256,256]{2,1,0:T(8,128)(2,1)S(1)}, bf16[8,256,256]{2,1,0:T(8,128)(2,1)S(1)}, u32[]{:S(2)}, u32[]{:S(2)}) %collective-permute-start.20) | collective-permute-done | bytes 1048608 | tf_op jit(solution)/shard_map/ppermute | solution.py:46
  127.4 0.4 add_convert_fusion
  127.9 11.7 %collective-permute-start.23 = (bf16[256,256]{1,0:T(8,128)(2,1)S(1)}, bf16[256,256]{1,0:T(8,128)(2,1)S(1)}, u32[]{:S(2)}, u32[]{:S(2)}) collective-permute-start(bf16[256,256]{1,0:T(8,128)(2,1)S(1)} %get-tuple-element.50), channel_id=1, source_target_pairs={{0,224},{32,0},{64,32},{96,64},{128,96},{160,128},{192,160},{224,1... | collective-permute-start | bytes 393224 | tf_op jit(solution)/shard_map/ppermute | solution.py:46
  139.5 1.5 collective-permute-start.24
  141.1 2.7 %collective-permute-done.23 = bf16[256,256]{1,0:T(8,128)(2,1)S(1)} collective-permute-done((bf16[256,256]{1,0:T(8,128)(2,1)S(1)}, bf16[256,256]{1,0:T(8,128)(2,1)S(1)}, u32[]{:S(2)}, u32[]{:S(2)}) %collective-permute-start.23) | collective-permute-done | bytes 131104 | tf_op jit(solution)/shard_map/ppermute | solution.py:46
  143.8 0.5 collective-permute-start.29
  144.2 2.1 %collective-permute-done.27 = bf16[256,256]{1,0:T(8,128)(2,1)S(1)} collective-permute-done((bf16[256,256]{1,0:T(8,128)(2,1)S(1)}, bf16[256,256]{1,0:T(8,128)(2,1)S(1)}, u32[]{:S(2)}, u32[]{:S(2)}) %collective-permute-start.27) | collective-permute-done | bytes 131104 | tf_op jit(solution)/shard_map/ppermute | solution.py:46
  146.3 1.3 collective-permute-start.26
  147.6 0.5 collective-permute-done.24
  148.2 4.2 %collective-permute-start.25 = (bf16[256,256]{1,0:T(8,128)(2,1)S(1)}, bf16[256,256]{1,0:T(8,128)(2,1)S(1)}, u32[]{:S(2)}, u32[]{:S(2)}) collective-permute-start(bf16[256,256]{1,0:T(8,128)(2,1)S(1)} %get-tuple-element.48), channel_id=1, source_target_pairs={{0,192},{32,224},{64,0},{96,32},{128,64},{160,96},{192,128},{224,1... | collective-permute-start | bytes 393224 | tf_op jit(solution)/shard_map/ppermute | solution.py:46
  152.4 1.1 finish.1
  153.4 0.7 collective-permute-done.26
  154.1 0.8 collective-permute-done.25
  154.9 5.7 %collective-permute-done.28 = bf16[256,256]{1,0:T(8,128)(2,1)S(1)} collective-permute-done((bf16[256,256]{1,0:T(8,128)(2,1)S(1)}, bf16[256,256]{1,0:T(8,128)(2,1)S(1)}, u32[]{:S(2)}, u32[]{:S(2)}) %collective-permute-start.28) | collective-permute-done | bytes 131104 | tf_op jit(solution)/shard_map/ppermute | solution.py:46
  160.8 0.6 slice.97
  161.4 0.6 fusion.3
  (43 shorter events, 1.1 us)
Async XLA Ops:
  0.6 46.1 %copy-start = (bf16[256,512]{1,0:T(8,128)(2,1)S(1)}, bf16[256,512]{1,0:T(8,128)(2,1)}, u32[]{:S(2)}) copy-start(bf16[256,512]{1,0:T(8,128)(2,1)} %param.5) | copy-start | bytes 786436
  1.5 45.4 %collective-permute-start.2 = (s32[8,128]{1,0:T(8,128)S(1)}, s32[8,128]{1,0:T(8,128)S(1)}, u32[]{:S(2)}, u32[]{:S(2)}) collective-permute-start(s32[8,128]{1,0:T(8,128)S(1)} %reshape.118), channel_id=1, source_target_pairs={{0,3},{1,0},{2,1},{3,2},{4,7},{5,4},{6,5},{7,6},{8,11},{9,8},{10,9... | collective-permute-start | bytes 12296 | tf_op jit(solution)/shard_map/ppermute | solution.py:46
  1.9 45.1 %collective-permute-start.1 = (s32[8,128]{1,0:T(8,128)S(1)}, s32[8,128]{1,0:T(8,128)S(1)}, u32[]{:S(2)}, u32[]{:S(2)}) collective-permute-start(s32[8,128]{1,0:T(8,128)S(1)} %reshape.118), channel_id=1, source_target_pairs={{0,2},{1,3},{2,0},{3,1},{4,6},{5,7},{6,4},{7,5},{8,10},{9,11},{10,... | collective-permute-start | bytes 12296 | tf_op jit(solution)/shard_map/ppermute | solution.py:46
  4.5 43.0 %collective-permute-start = (s32[8,128]{1,0:T(8,128)S(1)}, s32[8,128]{1,0:T(8,128)S(1)}, u32[]{:S(2)}, u32[]{:S(2)}) collective-permute-start(s32[8,128]{1,0:T(8,128)S(1)} %reshape.118), channel_id=1, source_target_pairs={{0,1},{1,2},{2,3},{3,0},{4,5},{5,6},{6,7},{7,4},{8,9},{9,10},{10,1... | collective-permute-start | bytes 12296 | tf_op jit(solution)/shard_map/ppermute | solution.py:46
  8.1 13.2 %collective-permute-start.4 = (bf16[256,256]{1,0:T(8,128)(2,1)S(1)}, bf16[256,256]{1,0:T(8,128)(2,1)S(1)}, u32[]{:S(2)}, u32[]{:S(2)}) collective-permute-start(bf16[256,256]{1,0:T(8,128)(2,1)S(1)} %constant_dynamic-update-slice_fusion), channel_id=1, source_target_pairs={{0,64},{32,96},{64,128},{96,160},{128,192},{160,224},{192,0},{224,... | collective-permute-start | bytes 393224 | tf_op jit(solution)/shard_map/ppermute | solution.py:46
  11.5 11.7 %collective-permute-start.3 = (bf16[256,256]{1,0:T(8,128)(2,1)S(1)}, bf16[256,256]{1,0:T(8,128)(2,1)S(1)}, u32[]{:S(2)}, u32[]{:S(2)}) collective-permute-start(bf16[256,256]{1,0:T(8,128)(2,1)S(1)} %constant_dynamic-update-slice_fusion), channel_id=1, source_target_pairs={{0,32},{32,64},{64,96},{96,128},{128,160},{160,192},{192,224},{224... | collective-permute-start | bytes 393224 | tf_op jit(solution)/shard_map/ppermute | solution.py:46
  21.3 8.8 %collective-permute-start.7 = (bf16[256,256]{1,0:T(8,128)(2,1)S(1)}, bf16[256,256]{1,0:T(8,128)(2,1)S(1)}, u32[]{:S(2)}, u32[]{:S(2)}) collective-permute-start(bf16[256,256]{1,0:T(8,128)(2,1)S(1)} %constant_dynamic-update-slice_fusion), channel_id=1, source_target_pairs={{0,192},{32,224},{64,0},{96,32},{128,64},{160,96},{192,128},{224,1... | collective-permute-start | bytes 393224 | tf_op jit(solution)/shard_map/ppermute | solution.py:46
  23.2 6.2 %collective-permute-start.5 = (bf16[256,256]{1,0:T(8,128)(2,1)S(1)}, bf16[256,256]{1,0:T(8,128)(2,1)S(1)}, u32[]{:S(2)}, u32[]{:S(2)}) collective-permute-start(bf16[256,256]{1,0:T(8,128)(2,1)S(1)} %collective-permute-done.4), channel_id=1, source_target_pairs={{0,32},{32,64},{64,96},{96,128},{128,160},{160,192},{192,224},{224... | collective-permute-start | bytes 393224 | tf_op jit(solution)/shard_map/ppermute | solution.py:46
  24.4 22.4 %copy-start.1 = (bf16[256,512]{1,0:T(8,128)(2,1)S(1)}, bf16[256,512]{1,0:T(8,128)(2,1)}, u32[]{:S(2)}) copy-start(bf16[256,512]{1,0:T(8,128)(2,1)} %param.8) | copy-start | bytes 786436
  29.4 7.2 %collective-permute-start.6 = (bf16[256,256]{1,0:T(8,128)(2,1)S(1)}, bf16[256,256]{1,0:T(8,128)(2,1)S(1)}, u32[]{:S(2)}, u32[]{:S(2)}) collective-permute-start(bf16[256,256]{1,0:T(8,128)(2,1)S(1)} %collective-permute-done.4), channel_id=1, source_target_pairs={{0,64},{32,96},{64,128},{96,160},{128,192},{160,224},{192,0},{224,... | collective-permute-start | bytes 393224 | tf_op jit(solution)/shard_map/ppermute | solution.py:46
  30.0 12.8 %collective-permute-start.9 = (bf16[256,256]{1,0:T(8,128)(2,1)S(1)}, bf16[256,256]{1,0:T(8,128)(2,1)S(1)}, u32[]{:S(2)}, u32[]{:S(2)}) collective-permute-start(bf16[256,256]{1,0:T(8,128)(2,1)S(1)} %constant_dynamic-update-slice_fusion), channel_id=1, source_target_pairs={{0,224},{32,0},{64,32},{96,64},{128,96},{160,128},{192,160},{224,1... | collective-permute-start | bytes 393224 | tf_op jit(solution)/shard_map/ppermute | solution.py:46
  36.6 5.0 %collective-permute-start.8 = (bf16[256,256]{1,0:T(8,128)(2,1)S(1)}, bf16[256,256]{1,0:T(8,128)(2,1)S(1)}, u32[]{:S(2)}, u32[]{:S(2)}) collective-permute-start(bf16[256,256]{1,0:T(8,128)(2,1)S(1)} %collective-permute-done.7), channel_id=1, source_target_pairs={{0,224},{32,0},{64,32},{96,64},{128,96},{160,128},{192,160},{224,1... | collective-permute-start | bytes 393224 | tf_op jit(solution)/shard_map/ppermute | solution.py:46
  43.5 23.4 %collective-permute-start.12 = (bf16[8,256,256]{2,1,0:T(8,128)(2,1)}, bf16[8,256,256]{2,1,0:T(8,128)(2,1)S(1)}, u32[]{:S(2)}, u32[]{:S(2)}) collective-permute-start(bf16[8,256,256]{2,1,0:T(8,128)(2,1)} %bitcast_dynamic-update-slice_fusion.refs_0_), channel_id=1, source_target_pairs={{0,24},{8,0},{16,8},{24,16},{1,25},{9,1},{17,9},{25,17},{2,26},{10... | collective-permute-start | bytes 3145736 | tf_op jit(solution)/shard_map/ppermute | solution.py:46
  44.4 22.9 %collective-permute-start.10 = (bf16[8,256,256]{2,1,0:T(8,128)(2,1)}, bf16[8,256,256]{2,1,0:T(8,128)(2,1)S(1)}, u32[]{:S(2)}, u32[]{:S(2)}) collective-permute-start(bf16[8,256,256]{2,1,0:T(8,128)(2,1)} %bitcast_dynamic-update-slice_fusion.refs_0_), channel_id=1, source_target_pairs={{0,8},{8,16},{16,24},{24,0},{1,9},{9,17},{17,25},{25,1},{2,10},{10... | collective-permute-start | bytes 3145736 | tf_op jit(solution)/shard_map/ppermute | solution.py:46
  46.9 32.4 %collective-permute-start.15 = (bf16[1024,128]{1,0:T(8,128)(2,1)S(1)}, bf16[1024,128]{1,0:T(8,128)(2,1)S(1)}, u32[]{:S(2)}, u32[]{:S(2)}) collective-permute-start(bf16[1024,128]{1,0:T(8,128)(2,1)S(1)} %bitcast.79), channel_id=1, source_target_pairs={{0,4},{4,0},{1,5},{5,1},{2,6},{6,2},{3,7},{7,3},{8,12},{12,8},{9,1... | collective-permute-start | bytes 786440 | tf_op jit(solution)/shard_map/ppermute | solution.py:46
  47.0 23.8 %collective-permute-start.14 = (bf16[1024,128]{1,0:T(8,128)(2,1)S(1)}, bf16[1024,128]{1,0:T(8,128)(2,1)S(1)}, u32[]{:S(2)}, u32[]{:S(2)}) collective-permute-start(bf16[1024,128]{1,0:T(8,128)(2,1)S(1)} %bitcast.72), channel_id=1, source_target_pairs={{0,4},{4,0},{1,5},{5,1},{2,6},{6,2},{3,7},{7,3},{8,12},{12,8},{9,1... | collective-permute-start | bytes 786440 | tf_op jit(solution)/shard_map/ppermute | solution.py:46
  67.0 12.4 %collective-permute-start.13 = (bf16[4,256,256]{2,1,0:T(8,128)(2,1)S(1)}, bf16[4,256,256]{2,1,0:T(8,128)(2,1)S(1)}, u32[]{:S(2)}, u32[]{:S(2)}) collective-permute-start(bf16[4,256,256]{2,1,0:T(8,128)(2,1)S(1)} %slice.66), channel_id=1, source_target_pairs={{0,24},{8,0},{16,8},{24,16},{1,25},{9,1},{17,9},{25,17},{2,26},{10... | collective-permute-start | bytes 1572872 | tf_op jit(solution)/shard_map/ppermute | solution.py:46
  67.3 12.1 %collective-permute-start.11 = (bf16[4,256,256]{2,1,0:T(8,128)(2,1)S(1)}, bf16[4,256,256]{2,1,0:T(8,128)(2,1)S(1)}, u32[]{:S(2)}, u32[]{:S(2)}) collective-permute-start(bf16[4,256,256]{2,1,0:T(8,128)(2,1)S(1)} %slice.65), channel_id=1, source_target_pairs={{0,8},{8,16},{16,24},{24,0},{1,9},{9,17},{17,25},{25,1},{2,10},{10... | collective-permute-start | bytes 1572872 | tf_op jit(solution)/shard_map/ppermute | solution.py:46
  81.6 1.3 collective-permute-start.16
  85.5 14.1 %collective-permute-start.21 = (bf16[4,256,256]{2,1,0:T(8,128)(2,1)S(1)}, bf16[4,256,256]{2,1,0:T(8,128)(2,1)S(1)}, u32[]{:S(2)}, u32[]{:S(2)}) collective-permute-start(bf16[4,256,256]{2,1,0:T(8,128)(2,1)S(1)} %get-tuple-element.47), channel_id=1, source_target_pairs={{0,8},{8,16},{16,24},{24,0},{1,9},{9,17},{17,25},{25,1},{2,10},{10... | collective-permute-start | bytes 1572872 | tf_op jit(solution)/shard_map/ppermute | solution.py:46
  85.6 15.8 %collective-permute-start.19 = (bf16[4,256,256]{2,1,0:T(8,128)(2,1)S(1)}, bf16[4,256,256]{2,1,0:T(8,128)(2,1)S(1)}, u32[]{:S(2)}, u32[]{:S(2)}) collective-permute-start(bf16[4,256,256]{2,1,0:T(8,128)(2,1)S(1)} %get-tuple-element.45), channel_id=1, source_target_pairs={{0,24},{8,0},{16,8},{24,16},{1,25},{9,1},{17,9},{25,17},{2,26},{10... | collective-permute-start | bytes 1572872 | tf_op jit(solution)/shard_map/ppermute | solution.py:46
  99.8 24.5 %collective-permute-start.22 = (bf16[8,256,256]{2,1,0:T(8,128)(2,1)S(1)}, bf16[8,256,256]{2,1,0:T(8,128)(2,1)S(1)}, u32[]{:S(2)}, u32[]{:S(2)}) collective-permute-start(bf16[8,256,256]{2,1,0:T(8,128)(2,1)S(1)} %pad_maximum_fusion.1), channel_id=1, source_target_pairs={{0,8},{8,16},{16,24},{24,0},{1,9},{9,17},{17,25},{25,1},{2,10},{10... | collective-permute-start | bytes 3145736 | tf_op jit(solution)/shard_map/ppermute | solution.py:46
  101.6 25.7 %collective-permute-start.20 = (bf16[8,256,256]{2,1,0:T(8,128)(2,1)S(1)}, bf16[8,256,256]{2,1,0:T(8,128)(2,1)S(1)}, u32[]{:S(2)}, u32[]{:S(2)}) collective-permute-start(bf16[8,256,256]{2,1,0:T(8,128)(2,1)S(1)} %pad_maximum_fusion), channel_id=1, source_target_pairs={{0,24},{8,0},{16,8},{24,16},{1,25},{9,1},{17,9},{25,17},{2,26},{10... | collective-permute-start | bytes 3145736 | tf_op jit(solution)/shard_map/ppermute | solution.py:46
  102.2 50.1 %collective-permute-start.17 = (f32[128,1024]{1,0:T(8,128)S(1)}, f32[128,1024]{1,0:T(8,128)S(1)}, u32[]{:S(2)}, u32[]{:S(2)}) collective-permute-start(f32[128,1024]{1,0:T(8,128)S(1)} %get-tuple-element.34), channel_id=1, source_target_pairs={{0,4},{4,0},{1,5},{5,1},{2,6},{6,2},{3,7},{7,3},{8,12},{12,8},{9,1... | collective-permute-start | bytes 1572872 | tf_op jit(solution)/shard_map/ppermute | solution.py:46
  108.4 44.0 %collective-permute-start.18 = (f32[128,1024]{1,0:T(8,128)S(1)}, f32[128,1024]{1,0:T(8,128)S(1)}, u32[]{:S(2)}, u32[]{:S(2)}) collective-permute-start(f32[128,1024]{1,0:T(8,128)S(1)} %get-tuple-element.40), channel_id=1, source_target_pairs={{0,4},{4,0},{1,5},{5,1},{2,6},{6,2},{3,7},{7,3},{8,12},{12,8},{9,1... | collective-permute-start | bytes 1572872 | tf_op jit(solution)/shard_map/ppermute | solution.py:46
  127.9 15.9 %collective-permute-start.23 = (bf16[256,256]{1,0:T(8,128)(2,1)S(1)}, bf16[256,256]{1,0:T(8,128)(2,1)S(1)}, u32[]{:S(2)}, u32[]{:S(2)}) collective-permute-start(bf16[256,256]{1,0:T(8,128)(2,1)S(1)} %get-tuple-element.50), channel_id=1, source_target_pairs={{0,224},{32,0},{64,32},{96,64},{128,96},{160,128},{192,160},{224,1... | collective-permute-start | bytes 393224 | tf_op jit(solution)/shard_map/ppermute | solution.py:46
  139.5 6.8 %collective-permute-start.27 = (bf16[256,256]{1,0:T(8,128)(2,1)S(1)}, bf16[256,256]{1,0:T(8,128)(2,1)S(1)}, u32[]{:S(2)}, u32[]{:S(2)}) collective-permute-start(bf16[256,256]{1,0:T(8,128)(2,1)S(1)} %get-tuple-element.52), channel_id=1, source_target_pairs={{0,32},{32,64},{64,96},{96,128},{128,160},{160,192},{192,224},{224... | collective-permute-start | bytes 393224 | tf_op jit(solution)/shard_map/ppermute | solution.py:46
  139.5 8.6 %collective-permute-start.24 = (bf16[256,256]{1,0:T(8,128)(2,1)S(1)}, bf16[256,256]{1,0:T(8,128)(2,1)S(1)}, u32[]{:S(2)}, u32[]{:S(2)}) collective-permute-start(bf16[256,256]{1,0:T(8,128)(2,1)S(1)} %get-tuple-element.54), channel_id=1, source_target_pairs={{0,192},{32,224},{64,0},{96,32},{128,64},{160,96},{192,128},{224,1... | collective-permute-start | bytes 393224 | tf_op jit(solution)/shard_map/ppermute | solution.py:46
  143.8 9.7 %collective-permute-start.29 = (bf16[256,256]{1,0:T(8,128)(2,1)S(1)}, bf16[256,256]{1,0:T(8,128)(2,1)S(1)}, u32[]{:S(2)}, u32[]{:S(2)}) collective-permute-start(bf16[256,256]{1,0:T(8,128)(2,1)S(1)} %get-tuple-element.51), channel_id=1, source_target_pairs={{0,32},{32,64},{64,96},{96,128},{128,160},{160,192},{192,224},{224... | collective-permute-start | bytes 393224 | tf_op jit(solution)/shard_map/ppermute | solution.py:46
  146.3 7.8 %collective-permute-start.26 = (bf16[256,256]{1,0:T(8,128)(2,1)S(1)}, bf16[256,256]{1,0:T(8,128)(2,1)S(1)}, u32[]{:S(2)}, u32[]{:S(2)}) collective-permute-start(bf16[256,256]{1,0:T(8,128)(2,1)S(1)} %get-tuple-element.53), channel_id=1, source_target_pairs={{0,224},{32,0},{64,32},{96,64},{128,96},{160,128},{192,160},{224,1... | collective-permute-start | bytes 393224 | tf_op jit(solution)/shard_map/ppermute | solution.py:46
  148.2 6.7 %collective-permute-start.25 = (bf16[256,256]{1,0:T(8,128)(2,1)S(1)}, bf16[256,256]{1,0:T(8,128)(2,1)S(1)}, u32[]{:S(2)}, u32[]{:S(2)}) collective-permute-start(bf16[256,256]{1,0:T(8,128)(2,1)S(1)} %get-tuple-element.48), channel_id=1, source_target_pairs={{0,192},{32,224},{64,0},{96,32},{128,64},{160,96},{192,128},{224,1... | collective-permute-start | bytes 393224 | tf_op jit(solution)/shard_map/ppermute | solution.py:46
  152.4 8.3 %collective-permute-start.28 = (bf16[256,256]{1,0:T(8,128)(2,1)S(1)}, bf16[256,256]{1,0:T(8,128)(2,1)S(1)}, u32[]{:S(2)}, u32[]{:S(2)}) collective-permute-start(bf16[256,256]{1,0:T(8,128)(2,1)S(1)} %get-tuple-element.49), channel_id=1, source_target_pairs={{0,64},{32,96},{64,128},{96,160},{128,192},{160,224},{192,0},{224,... | collective-permute-start | bytes 393224 | tf_op jit(solution)/shard_map/ppermute | solution.py:46
where the time goes:
time: 163 us; the launch traced here: 162 us
  waiting for transfers between devices  75.2 us (46%)
  starting transfers between devices  50 us (31%)
  Pallas kernels  25 us (15%)
  local copies, waits for them, and re-layouts  8.78 us (5%)
  other arithmetic  2.15 us (1%)
    ppermute x30, waiting for transfers between devices, shift(): return lax.ppermute(a, axis, [(i, (i + d) % n) for i in range(n)])  75.2 us
    ppermute x30, starting transfers between devices, shift(): return lax.ppermute(a, axis, [(i, (i + d) % n) for i in range(n)])  50 us
    pallas_call x3, Pallas kernels, backward(): pl.pallas_call(functools.partial(backward_kernel, base, sizes, first, bas...  13.2 us
    pallas_call x3, Pallas kernels, forward(): pl.pallas_call(functools.partial(forward_kernel, base, sizes, first, last...  10.8 us
    unnamed x12, local copies, waits for them, and re-layouts  5.44 us
  transfers between devices with their start and end apart: 30, of which 15 were waited for; matrix products, arithmetic and copies ran while one was open for 5% of the time, Pallas kernels for 12%

commit v1 on v0

--- a/solution.py
+++ b/solution.py
@@ -25,12 +25,12 @@
 NT = (((1,), (1,)), ((), ()))
 NN = (((1,), (0,)), ((), ()))
 CORE_AT = 32
+QUAD = 4
 VMEM_LIMIT = 40 * 1024 * 1024
 STAT = (2, 3, COLS)
 ACC = (HEAD_DIM, COLS)
-ROWS = (COLS, HEAD_DIM)
+PAIR = (2, COLS, HEAD_DIM)
 PIECE = (HALF, 2 * HEAD_DIM)
-SLOT_FLOPS = 2 * HALF * 2 * COLS * HEAD_DIM
 
 
 def dot(a, b, dims):
@@ -52,27 +52,27 @@
     return (i - j) <= off
 
 
-def fetch(i, kv_refs, sizes, kv_buf):
-    if len(kv_refs) == 1:
-        return kv_refs[0][0]
-
-    @pl.when(i < sizes[0])
-    def _():
-        kv_buf[...] = kv_refs[0][0]
-
-    @pl.when(i >= sizes[0])
-    def _():
-        kv_buf[...] = kv_refs[1][0]
+def fetch(i, kv_refs, kv_buf):
+    for a, ref in enumerate(kv_refs):
+
+        @pl.when(i // QUAD == a)
+        def _():
+            kv_buf[...] = ref[0]
 
     return kv_buf[...]
 
 
-def forward_kernel(base, sizes, first, last, info, *refs):
-    n = len(sizes)
+def query_refs(refs):
+    return [ref.at[0] for ref in refs]
+
+
+def grad_refs(refs):
+    return [ref.at[1] for ref in refs]
+
+
+def forward_kernel(base, n, first, last, info, *refs):
     kv_refs, refs = refs[:n], refs[n:]
-    q_refs, refs = refs[:2], refs[2:]
-    if last:
-        g_refs, refs = refs[:2], refs[2:]
+    q_refs, g_refs, refs = query_refs(refs[:2]), grad_refs(refs[:2]), refs[2:]
     if not first:
         stat_in, acc_in, refs = refs[0], refs[1:3], refs[3:]
     stat_ref, acc_refs, (s_ref, p_ref, kv_buf) = refs[0], refs[1:3], refs[3:]
@@ -92,7 +92,7 @@
                 acc_refs[half][...] = acc_in[half][...]
 
     def step(masked):
-        kv = fetch(i, kv_refs, sizes, kv_buf)
+        kv = fetch(i, kv_refs, kv_buf)
         k = kv[:, :HEAD_DIM]
         vt = jnp.transpose(kv[:, HEAD_DIM:])
         for half in range(2):
@@ -125,7 +125,7 @@
 
     if last:
 
-        @pl.when(i == sum(sizes) - 1)
+        @pl.when(i == QUAD * n - 1)
         def _():
             eye = (
                 lax.broadcasted_iota(jnp.int32, (HEAD_DIM, HEAD_DIM), 0)
@@ -146,10 +146,10 @@
     return m + jnp.log2(total), e0 / total, e1 / total
 
 
-def backward_kernel(base, sizes, first, masks, info, *refs):
-    n = len(sizes)
+def backward_kernel(base, n, first, masks, info, *refs):
     kv_refs, refs = refs[:n], refs[n:]
-    q_refs, g_refs, mine, other, refs = refs[:2], refs[2:4], refs[4], refs[5], refs[6:]
+    q_refs, g_refs, refs = query_refs(refs[:2]), grad_refs(refs[:2]), refs[2:]
+    mine, other, refs = refs[0], refs[1], refs[2:]
     if not first:
         dq_in, refs = refs[:2], refs[2:]
     dq_refs, out_refs, refs = refs[:2], refs[2 : 2 + n], refs[2 + n :]
@@ -166,7 +166,7 @@
             dq_refs[half][...] = jnp.zeros(ACC, F32) if first else dq_in[half][...]
 
     def step(masked):
-        kv = fetch(i, kv_refs, sizes, kv_buf)
+        kv = fetch(i, kv_refs, kv_buf)
         k = kv[:, :HEAD_DIM]
         v = kv[:, HEAD_DIM:]
         kt = jnp.transpose(k)
@@ -206,17 +206,11 @@
     def _():
         out_buf[...] = jnp.zeros(PIECE, BF)
 
-    if n == 1:
-        out_refs[0][0] = out_buf[...]
-    else:
-
-        @pl.when(i < sizes[0])
+    for a, ref in enumerate(out_refs):
+
+        @pl.when(i // QUAD == a)
         def _():
-            out_refs[0][0] = out_buf[...]
-
-        @pl.when(i >= sizes[0])
-        def _():
-            out_refs[1][0] = out_buf[...]
+            ref[0] = out_buf[...]
 
 
 def finish_kernel(mine, other, acc_mine, acc_other, dq_mine, dq_other, att_ref, dq_ref):
@@ -233,36 +227,29 @@
     return pl.BlockSpec(shape, lambda i, info: (0,) * len(shape))
 
 
-def piece_specs(sizes):
-    block = (1,) + PIECE
-    if len(sizes) == 1:
-        return [pl.BlockSpec(block, lambda i, info: (i, 0, 0))]
-    n = sizes[0]
-    return [
-        pl.BlockSpec(block, lambda i, info: (jnp.minimum(i, n - 1), 0, 0)),
-        pl.BlockSpec(block, lambda i, info: (jnp.maximum(i - n, 0), 0, 0)),
-    ]
-
-
-def cost(slots, products):
-    return pl.CostEstimate(
-        flops=slots * products * SLOT_FLOPS, bytes_accessed=1 << 22, transcendentals=slots * HALF * 2 * COLS
-    )
-
-
-def forward(base, info, kvs, q, state, g):
-    sizes = [a.shape[0] for a in kvs]
+def piece_specs(n):
+    def spec(a):
+        return pl.BlockSpec((1,) + PIECE, lambda i, info: (jnp.clip(i - QUAD * a, 0, QUAD - 1), 0, 0))
+
+    return [spec(a) for a in range(n)]
+
+
+def cost(flops):
+    return pl.CostEstimate(flops=flops, bytes_accessed=1 << 16, transcendentals=0)
+
+
+def forward(base, info, kvs, qg, state, last):
+    n = len(kvs)
     first = state is None
-    last = g is not None
-    ins = list(kvs) + list(q) + (list(g) if last else []) + ([] if first else list(state))
-    specs = piece_specs(sizes) + [whole(ROWS)] * (4 if last else 2)
+    ins = list(kvs) + list(qg) + ([] if first else list(state))
+    specs = piece_specs(n) + [whole(PAIR)] * 2
     if not first:
         specs += [whole(STAT), whole(ACC), whole(ACC)]
     return pl.pallas_call(
-        functools.partial(forward_kernel, base, sizes, first, last),
+        functools.partial(forward_kernel, base, n, first, last),
         grid_spec=pltpu.PrefetchScalarGridSpec(
             num_scalar_prefetch=1,
-            grid=(sum(sizes),),
+            grid=(QUAD * n,),
             in_specs=specs,
             out_specs=[whole(STAT), whole(ACC), whole(ACC)],
             scratch_shapes=[
@@ -273,26 +260,26 @@
         ),
         out_shape=[jax.ShapeDtypeStruct(s, F32) for s in (STAT, ACC, ACC)],
         compiler_params=pltpu.CompilerParams(vmem_limit_bytes=VMEM_LIMIT),
-        cost_estimate=cost(3, 2),
+        cost_estimate=cost(200_000_000),
         name="forward",
     )(info, *ins)
 
 
-def backward(base, info, kvs, q, g, mine, other, dq):
-    sizes = [a.shape[0] for a in kvs]
+def backward(base, info, kvs, qg, mine, other, dq):
+    n = len(kvs)
     first = dq is None
-    ins = list(kvs) + list(q) + list(g) + [mine, other] + ([] if first else list(dq))
-    specs = piece_specs(sizes) + [whole(ROWS)] * 4 + [whole(STAT)] * 2
+    ins = list(kvs) + list(qg) + [mine, other] + ([] if first else list(dq))
+    specs = piece_specs(n) + [whole(PAIR)] * 2 + [whole(STAT)] * 2
     if not first:
         specs += [whole(ACC), whole(ACC)]
     wide_shape = (HALF, 2 * COLS)
     res = pl.pallas_call(
-        functools.partial(backward_kernel, base, sizes, first, base == 0),
+        functools.partial(backward_kernel, base, n, first, base == 0),
         grid_spec=pltpu.PrefetchScalarGridSpec(
             num_scalar_prefetch=1,
-            grid=(sum(sizes),),
+            grid=(QUAD * n,),
             in_specs=specs,
-            out_specs=[whole(ACC), whole(ACC)] + piece_specs(sizes),
+            out_specs=[whole(ACC), whole(ACC)] + piece_specs(n),
             scratch_shapes=[
                 pltpu.VMEM((2, 2, COLS), F32),
                 pltpu.VMEM(wide_shape, F32),
@@ -305,7 +292,7 @@
         ),
         out_shape=[jax.ShapeDtypeStruct(ACC, F32)] * 2 + [jax.ShapeDtypeStruct(a.shape, BF) for a in kvs],
         compiler_params=pltpu.CompilerParams(vmem_limit_bytes=VMEM_LIMIT),
-        cost_estimate=cost(3, 5),
+        cost_estimate=cost(200_000_000),
         name="backward",
     )(info, *ins)
     return res[:2], res[2:]
@@ -317,17 +304,107 @@
         finish_kernel,
         out_shape=[shape, shape],
         compiler_params=pltpu.CompilerParams(vmem_limit_bytes=VMEM_LIMIT),
-        cost_estimate=pl.CostEstimate(flops=1 << 20, bytes_accessed=1 << 22, transcendentals=0),
+        cost_estimate=pl.CostEstimate(flops=1 << 20, bytes_accessed=1 << 16, transcendentals=0),
         name="finish",
     )(mine, other, acc_mine, acc_other, dq_mine, dq_other)
 
 
-def plan(gate_score):
+def join_kernel(k_ref, v_ref, out_ref):
+    out_ref[:, :HEAD_DIM] = k_ref[...]
+    out_ref[:, HEAD_DIM:] = v_ref[...]
+
+
+def join(k, v):
+    return pl.pallas_call(join_kernel, out_shape=jax.ShapeDtypeStruct(PIECE, BF), name="join")(k, v)
+
+
+def prepare_kernel(query, grad_out, gate, after, qg_ref, gate_ref):
+    for h in range(GROUP):
+        rows = slice(h * HALF, (h + 1) * HALF)
+        cols = slice(h * HEAD_DIM, (h + 1) * HEAD_DIM)
+        qg_ref[0, rows, :] = query[:, cols]
+        qg_ref[1, rows, :] = grad_out[:, cols]
+    gate_ref[...] = gate[...]
+
+
+def prepare(query, grad_out, gate, after):
+    ins = pl.BlockSpec(memory_space=pltpu.VMEM)
+    return pl.pallas_call(
+        prepare_kernel,
+        in_specs=[ins, ins, ins, pl.BlockSpec(memory_space=pl.ANY)],
+        out_shape=[jax.ShapeDtypeStruct(PAIR, BF), jax.ShapeDtypeStruct(gate.shape, jnp.int32)],
+        cost_estimate=cost(100_000_000),
+        name="prepare",
+    )(query, grad_out, gate, after)
+
+
+def stack_kernel(*refs):
+    for i in range(QUAD):
+        refs[-1][i] = refs[i][...]
+
+
+def stack(*pieces):
+    return pl.pallas_call(stack_kernel, out_shape=jax.ShapeDtypeStruct((QUAD,) + PIECE, BF), name="stack")(*pieces)
+
+
+def sum_high_kernel(own, one, three, keep, near_up, near_down, far):
+    def total(i):
+        return wide(own[i]) + wide(one[i]) + wide(three[i])
+
+    keep[...] = total(0)
+    near_down[...] = total(1).astype(BF)
+    near_up[...] = total(2).astype(BF)
+    far[...] = total(3).astype(BF)
+
+
+def sum_high(own, one, three):
+    shape = jax.ShapeDtypeStruct(PIECE, BF)
+    return pl.pallas_call(
+        sum_high_kernel,
+        out_shape=[jax.ShapeDtypeStruct(PIECE, F32), shape, shape, shape],
+        cost_estimate=cost(100_000_000),
+        name="sum_high",
+    )(own, one, three)
+
+
+def sum_low_kernel(own, one, three, keep, down, far, up, own_out, near_down, near_up, two_down, two_up):
+    def total(i):
+        return wide(own[i]) + wide(one[i]) + wide(three[i])
+
+    own_out[...] = total(0)
+    near_down[...] = total(1).astype(BF)
+    near_up[...] = total(2).astype(BF)
+    two_down[...] = (total(3) + wide(down[...]) + wide(far[...])).astype(BF)
+    two_up[...] = (keep[...] + wide(up[...])).astype(BF)
+
+
+def sum_low(own, one, three, keep, down, far, up):
+    shape = jax.ShapeDtypeStruct(PIECE, BF)
+    return pl.pallas_call(
+        sum_low_kernel,
+        out_shape=[jax.ShapeDtypeStruct(PIECE, F32), shape, shape, shape, shape],
+        cost_estimate=cost(100_000_000),
+        name="sum_low",
+    )(own, one, three, keep, down, far, up)
+
+
+def close_kernel(own, a, b, c, d, dk_ref, dv_ref):
+    total = own[...] + wide(a[...]) + wide(b[...]) + wide(c[...]) + wide(d[...])
+    dk_ref[...] = (total[:, :HEAD_DIM] * SCALE).astype(BF)
+    dv_ref[...] = total[:, HEAD_DIM:].astype(BF)
+
+
+def close(own, parts):
+    shape = jax.ShapeDtypeStruct((HALF, HEAD_DIM), BF)
+    return pl.pallas_call(close_kernel, out_shape=[shape, shape], name="close")(own, *parts)
+
+
+def plan(gate):
     z = lax.axis_index("z")
     x = lax.axis_index("x")
     own = z * 4 + x
-    mine = lax.optimization_barrier(gate_score.reshape(8, 128))
-    totals = mine + shift(mine, "head", 1) + shift(mine, "head", 2) + shift(mine, "head", 3)
+    totals = gate + lax.ppermute(gate, "head", [(0, 1), (1, 0), (2, 3), (3, 2)])
+    totals = totals + lax.ppermute(totals, "head", [(0, 2), (2, 0), (1, 3), (3, 1)])
     row = lax.dynamic_slice_in_dim(totals.reshape(NBLK, NBLK), own, 1, 0)[0]
     columns = jnp.arange(NBLK, dtype=jnp.int32)
     ranked = jnp.where(columns < own, row * NBLK + columns, -1)
@@ -335,64 +412,54 @@
     used = ((rank < TOPK) & (ranked >= 0)) | (columns == own)
     dz = (z - columns // 4) % 8
     dx = (x - columns % 4) % 4
-    group = jnp.where(dx < 2, dx, 5 - dx)
-    place = group * 8 + dz
+    pos = jnp.where(dz == 0, 0, jnp.where(dz <= 4, 2 * dz - 1, 2 * (8 - dz)))
+    side = 8 + 4 * (dx // 2) + jnp.where(pos < QUAD, pos, pos + QUAD)
+    place = jnp.where(dx == 0, pos, jnp.where(dx == 2, 24 + pos, side))
     live = jnp.sum((place[None, :] == columns[:, None]) & used[None, :], axis=1, dtype=jnp.int32)
     return jnp.concatenate([live, lax.axis_index("core")[None]])
 
 
-def heads_first(a):
-    return jnp.transpose(a.reshape(HALF, GROUP, HEAD_DIM), (1, 0, 2)).reshape(ROWS)
-
-
-def gather_z(piece):
+def on_device(query, key, value, grad_out, gate_score):
+    swap = functools.partial(shift, axis="core", d=1)
+    piece = join(key, value)
     a1, b1 = shift(piece, "z", 1), shift(piece, "z", -1)
     a2, b2 = shift(piece, "z", 2), shift(piece, "z", -2)
     a3, b3, a4 = shift(a2, "z", 1), shift(b2, "z", -1), shift(a2, "z", 2)
-    return jnp.stack([piece, a1, a2, a3, a4, b3, b2, b1])
-
-
-def scatter_z(t):
-    a = shift(t[3], "z", -1)
-    b = shift(t[4], "z", -2)
-    c = shift(t[5], "z", 1)
-    t2 = (wide(t[2]) + wide(a) + wide(b)).astype(BF)
-    t6 = (wide(t[6]) + wide(c)).astype(BF)
-    parts = [shift(t2, "z", -2), shift(t[1], "z", -1), shift(t6, "z", 2), shift(t[7], "z", 1)]
-    return wide(t[0]) + sum(wide(a) for a in parts)
-
-
-def on_device(query, key, value, grad_out, gate_score):
-    swap = functools.partial(shift, axis="core", d=1)
-    kv0 = gather_z(jnp.concatenate([key, value], axis=1))
-    q = heads_first(query)
-    g = heads_first(grad_out)
-    q = (q, swap(q))
-    g = (g, swap(g))
-    info = plan(gate_score)
-
-    kv1 = shift(kv0, "x", 1)
-    kv3 = shift(kv0, "x", -1)
-    kv2 = (shift(kv1[:4], "x", 1), shift(kv3[4:], "x", -1))
-
-    state = forward(0, info, [kv0], q, None, None)
-    state = forward(8, info, [kv1, kv3], q, state, None)
-    mine, acc, acc_away = forward(24, info, kv2, q, state, g)
+    low0 = stack(piece, a1, b1, a2)
+    high0 = stack(b2, a3, b3, a4)
+    low1, low3 = shift(low0, "x", 1), shift(low0, "x", -1)
+    high1, high3 = shift(high0, "x", 1), shift(high0, "x", -1)
+    low2, high2 = shift(low1, "x", 1), shift(high3, "x", -1)
+
+    qg, gate = prepare(query, grad_out, gate_score.reshape(8, 128), a3)
+    info = plan(gate)
+    qg = (qg, swap(qg))
+
+    state = forward(0, info, [low0, high0], qg, None, False)
+    state = forward(8, info, [low1, low3, high1, high3], qg, state, False)
+    mine, acc, acc_away = forward(24, info, [low2, high2], qg, state, True)
     other = swap(mine)
     acc_other = swap(acc_away)
 
-    dq, (low, high) = backward(24, info, kv2, q, g, mine, other, None)
-    low = shift(low, "x", -1)
-    high = shift(high, "x", 1)
-    dq, (t1, t3) = backward(8, info, [kv1, kv3], q, g, mine, other, dq)
-    t1 = jnp.concatenate([(wide(t1[:4]) + wide(low)).astype(BF), t1[4:]])
-    t3 = jnp.concatenate([t3[:4], (wide(t3[4:]) + wide(high)).astype(BF)])
-    t1 = shift(t1, "x", -1)
-    t3 = shift(t3, "x", 1)
-    dq, (t0,) = backward(0, info, [kv0], q, g, mine, other, dq)
-    total = scatter_z((wide(t0) + wide(t1) + wide(t3)).astype(BF))
-    grad_key = (total[:, :HEAD_DIM] * SCALE).astype(BF)
-    grad_value = total[:, HEAD_DIM:].astype(BF)
+    dq, (low2, high2) = backward(24, info, [low2, high2], qg, mine, other, None)
+    low2 = shift(low2, "x", -1)
+    high2 = shift(high2, "x", 1)
+    dq, (low1, low3, high1, high3) = backward(8, info, [low1, low3, high1, high3], qg, mine, other, dq)
+    high1, low3 = shift(high1, "x", -1), shift(low3, "x", 1)
+    high3 = shift((wide(high3) + wide(high2)).astype(BF), "x", 1)
+    low1 = shift((wide(low1) + wide(low2)).astype(BF), "x", -1)
+    dq, (low0, high0) = backward(0, info, [low0, high0], qg, mine, other, dq)
+
+    keep, up, down, far = sum_high(high0, high1, high3)
+    down, far, up = shift(down, "z", -1), shift(far, "z", -2), shift(up, "z", 1)
+    own, near_down, near_up, two_down, two_up = sum_low(low0, low1, low3, keep, down, far, up)
+    parts = [
+        shift(two_up, "z", 2),
+        shift(two_down, "z", -2),
+        shift(near_down, "z", -1),
+        shift(near_up, "z", 1),
+    ]
+    grad_key, grad_value = close(own, parts)
     attended, grad_query = finish(mine, other, acc, acc_other, dq[0], swap(dq[1]))
     return (attended, grad_query, grad_key, grad_value)
 

time: 163 us -> 151 us (0.926)
  the two profiles are of different devices: /device:TPU:14 before, /device:TPU:1 now
where the time goes in v1:
time: 151 us; the launch traced here: 148 us
  starting transfers between devices  66.2 us (44%)
  waiting for transfers between devices  44.2 us (29%)
  Pallas kernels  27.5 us (18%)
  local copies, waits for them, and re-layouts  7.98 us (5%)
    ppermute x30, starting transfers between devices, shift(): return lax.ppermute(a, axis, [(i, (i + d) % n) for i in range(n)])  62 us
    ppermute x30, waiting for transfers between devices, shift(): return lax.ppermute(a, axis, [(i, (i + d) % n) for i in range(n)])  42.6 us
    pallas_call x3, Pallas kernels, backward(): pl.pallas_call(functools.partial(backward_kernel, base, n, first, base ==...  7.52 us
    unnamed x54, local copies, waits for them, and re-layouts  7.24 us
    pallas_call x3, Pallas kernels, forward(): pl.pallas_call(functools.partial(forward_kernel, base, n, first, last), g...  4.97 us
    pallas_call x2, Pallas kernels, stack(): pl.pallas_call(stack_kernel, out_shape=jax.ShapeDtypeStruct((QUAD,) + PIE...  3.88 us
  transfers between devices with their start and end apart: 32, of which 14 were waited for; matrix products, arithmetic and copies ran while one was open for 2% of the time, Pallas kernels for 14%

profile of v1, /device:TPU:1, one launch (start us, length us, event | category | flops | bytes accessed | tf_op | source)
XLA Modules:
  0.0 148.4 jit_solution(814243299311877361)
XLA Ops:
  0.6 1.5 %join.1.refs_0_ = bf16[256,256]{1,0:T(8,128)(2,1)} custom-call(bf16[256,128]{1,0:T(8,128)(2,1)} %k_ref.1, bf16[256,128]{1,0:T(8,128)(2,1)} %v_ref.1), custom_call_target="tpu_custom_call" | custom-call | tf_op jit(solution)/shard_map/join/pallas_call | solution.py:318
  2.2 6.8 %collective-permute-start.8 = (bf16[256,256]{1,0:T(8,128)(2,1)}, bf16[256,256]{1,0:T(8,128)(2,1)S(1)}, u32[]{:S(2)}, u32[]{:S(2)}) collective-permute-start(bf16[256,256]{1,0:T(8,128)(2,1)} %join.1.refs_0_), channel_id=1, source_target_pairs={{0,192},{32,224},{64,0},{96,32},{128,64},{160,96},{192,128},{224,1... | collective-permute-start | bytes 393224 | tf_op jit(solution)/shard_map/ppermute | solution.py:46
  9.0 3.1 %collective-permute-start.5 = (bf16[256,256]{1,0:T(8,128)(2,1)}, bf16[256,256]{1,0:T(8,128)(2,1)S(1)}, u32[]{:S(2)}, u32[]{:S(2)}) collective-permute-start(bf16[256,256]{1,0:T(8,128)(2,1)} %join.1.refs_0_), channel_id=1, source_target_pairs={{0,224},{32,0},{64,32},{96,64},{128,96},{160,128},{192,160},{224,1... | collective-permute-start | bytes 393224 | tf_op jit(solution)/shard_map/ppermute | solution.py:46
  12.2 0.4 collective-permute-done.8.refs_0_
  12.6 4.7 %collective-permute-start.9 = (bf16[256,256]{1,0:T(8,128)(2,1)S(1)}, bf16[256,256]{1,0:T(8,128)(2,1)S(1)}, u32[]{:S(2)}, u32[]{:S(2)}) collective-permute-start(bf16[256,256]{1,0:T(8,128)(2,1)S(1)} %collective-permute-done.8.refs_0_), channel_id=1, source_target_pairs={{0,224},{32,0},{64,32},{96,64},{128,96},{160,128},{192,160},{224,1... | collective-permute-start | bytes 393224 | tf_op jit(solution)/shard_map/ppermute | solution.py:46
  17.4 1.4 collective-permute-start.1
  18.8 2.6 %collective-permute-done.4.refs_1_ = bf16[256,256]{1,0:T(8,128)(2,1)S(1)} collective-permute-done((bf16[256,256]{1,0:T(8,128)(2,1)}, bf16[256,256]{1,0:T(8,128)(2,1)S(1)}, u32[]{:S(2)}, u32[]{:S(2)}) %collective-permute-start.4) | collective-permute-done | bytes 131104 | tf_op jit(solution)/shard_map/ppermute | solution.py:46
  21.4 0.7 copy-done.24
  22.0 1.9 %stack.2.refs_0_ = bf16[4,256,256]{2,1,0:T(8,128)(2,1)} custom-call(bf16[256,256]{1,0:T(8,128)(2,1)} %join.1.refs_0_, bf16[256,256]{1,0:T(8,128)(2,1)} %copy-done.24, bf16[256,256]{1,0:T(8,128)(2,1)} %copy-done.23, bf16[256,256]{1,0:T(8,128)(2,1)} %copy-done.20), custom_call_target="tpu_custom_call" | custom-call | tf_op jit(solution)/shard_map/stack/pallas_call | solution.py:347
  24.0 1.2 collective-permute-start.6
  25.2 3.8 %collective-permute-done.1.after.refs_1_ = bf16[256,256]{1,0:T(8,128)(2,1)S(1)} collective-permute-done((bf16[256,256]{1,0:T(8,128)(2,1)S(1)}, bf16[256,256]{1,0:T(8,128)(2,1)S(1)}, u32[]{:S(2)}, u32[]{:S(2)}) %collective-permute-start.1) | collective-permute-done | bytes 131104 | tf_op jit(solution)/shard_map/ppermute | solution.py:46
  29.0 0.7 copy-done.11
  29.6 1.9 %stack.3.refs_1_ = bf16[4,256,256]{2,1,0:T(8,128)(2,1)} custom-call(bf16[256,256]{1,0:T(8,128)(2,1)} %copy-done.19, bf16[256,256]{1,0:T(8,128)(2,1)} %copy-done.11, bf16[256,256]{1,0:T(8,128)(2,1)} %copy-done.21, bf16[256,256]{1,0:T(8,128)(2,1)} %copy-done.22), custom_call_target="tpu_custom_call" | custom-call | tf_op jit(solution)/shard_map/stack/pallas_call | solution.py:347
  31.6 2.5 %collective-permute-start.11 = (bf16[4,256,256]{2,1,0:T(8,128)(2,1)}, bf16[4,256,256]{2,1,0:T(8,128)(2,1)S(1)}, u32[]{:S(2)}, u32[]{:S(2)}) collective-permute-start(bf16[4,256,256]{2,1,0:T(8,128)(2,1)} %stack.3.refs_1_), channel_id=1, source_target_pairs={{0,24},{8,0},{16,8},{24,16},{1,25},{9,1},{17,9},{25,17},{2,26},{10... | collective-permute-start | bytes 1572872 | tf_op jit(solution)/shard_map/ppermute | solution.py:46
  34.1 0.7 reshape.129.gate
  34.7 1.9 %prepare.1 = (bf16[2,1024,128]{2,1,0:T(8,128)(2,1)}, s32[8,128]{1,0:T(8,128)}) custom-call(bf16[256,512]{1,0:T(8,128)(2,1)} %query.1, bf16[256,512]{1,0:T(8,128)(2,1)} %grad_out.1, s32[8,128]{1,0:T(8,128)} %reshape.129.gate, bf16[256,256]{1,0:T(8,128)(2,1)} %copy-done.11), custom_call_target="tpu_custom_call" | custom-call | flops 100000000 | bytes 65536 | tf_op jit(solution)/shard_map/prepare/pallas_call | solution.py:332
  36.7 1.3 collective-permute-start.2
  38.0 1.7 %collective-permute-done.2 = s32[8,128]{1,0:T(8,128)S(1)} collective-permute-done((s32[8,128]{1,0:T(8,128)}, s32[8,128]{1,0:T(8,128)S(1)}, u32[]{:S(2)}, u32[]{:S(2)}) %collective-permute-start.2) | collective-permute-done | bytes 4128 | tf_op jit(solution)/shard_map/ppermute | solution.py:406
  39.6 2.9 %collective-permute-start.3 = (s32[8,128]{1,0:T(8,128)S(1)}, s32[8,128]{1,0:T(8,128)S(1)}, u32[]{:S(2)}, u32[]{:S(2)}) collective-permute-start(s32[8,128]{1,0:T(8,128)S(1)} %add.110), channel_id=1, source_target_pairs={{0,2},{2,0},{1,3},{3,1},{4,6},{6,4},{5,7},{7,5},{8,10},{10,8},{9,1... | collective-permute-start | bytes 12296 | tf_op jit(solution)/shard_map/ppermute | solution.py:407
  42.6 0.6 collective-permute-start.14
  43.2 0.9 collective-permute-start.15
  44.1 4.0 %collective-permute-start.13 = (bf16[2,1024,128]{2,1,0:T(8,128)(2,1)}, bf16[2,1024,128]{2,1,0:T(8,128)(2,1)S(1)}, u32[]{:S(2)}, u32[]{:S(2)}) collective-permute-start(bf16[2,1024,128]{2,1,0:T(8,128)(2,1)} %get-tuple-element.43.refs_2_.refs_4_), channel_id=1, source_target_pairs={{0,4},{4,0},{1,5},{5,1},{2,6},{6,2},{3,7},{7,3},{8,12},{12,8},{9,1... | collective-permute-start | bytes 1572872 | tf_op jit(solution)/shard_map/ppermute | solution.py:46
  48.3 2.7 %collective-permute-start.12 = (bf16[4,256,256]{2,1,0:T(8,128)(2,1)S(1)}, bf16[4,256,256]{2,1,0:T(8,128)(2,1)S(1)}, u32[]{:S(2)}, u32[]{:S(2)}) collective-permute-start(bf16[4,256,256]{2,1,0:T(8,128)(2,1)S(1)} %collective-permute-done.11.refs_3_), channel_id=1, source_target_pairs={{0,24},{8,0},{16,8},{24,16},{1,25},{9,1},{17,9},{25,17},{2,26},{10... | collective-permute-start | bytes 1572872 | tf_op jit(solution)/shard_map/ppermute | solution.py:46
  51.0 0.2 convert_reduce_fusion.1
  51.4 1.1 copy-done
  52.5 1.0 copy-done.2
  53.5 1.9 %forward.3 = (f32[2,3,1024]{2,1,0:T(4,128)S(1)}, f32[128,1024]{1,0:T(8,128)S(1)}, f32[128,1024]{1,0:T(8,128)S(1)}) custom-call(s32[33]{0:T(128)S(1)} %pad_add_fusion.info, bf16[4,256,256]{2,1,0:T(8,128)(2,1)S(1)} %copy-done.1, bf16[4,256,256]{2,1,0:T(8,128)(2,1)S(1)} %copy-done.2, bf16[2,1024,128]{2,1,0:T(8,128)(2,1)S(1)} %copy-done, ...), custom_call_target="tpu_custom_call" | custom-call | flops 200000000 | bytes 65536 | tf_op jit(solution)/shard_map/forward/pallas_call | solution.py:248
  55.4 1.1 forward.4
  56.5 9.1 %collective-permute-done.7.refs_0_ = bf16[4,256,256]{2,1,0:T(8,128)(2,1)S(1)} collective-permute-done((bf16[4,256,256]{2,1,0:T(8,128)(2,1)S(1)}, bf16[4,256,256]{2,1,0:T(8,128)(2,1)S(1)}, u32[]{:S(2)}, u32[]{:S(2)}) %collective-permute-start.7) | collective-permute-done | bytes 524320 | tf_op jit(solution)/shard_map/ppermute | solution.py:46
  65.6 0.7 collective-permute-done.12.refs_1_
  66.3 2.0 %forward.5 = (f32[2,3,1024]{2,1,0:T(4,128)S(1)}, f32[128,1024]{1,0:T(8,128)S(1)}, f32[128,1024]{1,0:T(8,128)}) custom-call(s32[33]{0:T(128)S(1)} %pad_add_fusion.info, bf16[4,256,256]{2,1,0:T(8,128)(2,1)S(1)} %collective-permute-done.7.refs_0_, bf16[4,256,256]{2,1,0:T(8,128)(2,1)S(1)} %collective-permute-done.12.refs_1_, bf16[2,1024,128]{2,1,0:T(8,128)(2,1)S(1)} %copy-done, ...), custom_call_target="tpu_custom_call" | custom-call | flops 200000000 | bytes 65536 | tf_op jit(solution)/shard_map/forward/pallas_call | solution.py:248
  68.2 4.0 %collective-permute-start.16 = (f32[2,3,1024]{2,1,0:T(4,128)S(1)}, f32[2,3,1024]{2,1,0:T(4,128)S(1)}, u32[]{:S(2)}, u32[]{:S(2)}) collective-permute-start(f32[2,3,1024]{2,1,0:T(4,128)S(1)} %get-tuple-element.50.refs_4_.refs_6_.mine), channel_id=1, source_target_pairs={{0,4},{4,0},{1,5},{5,1},{2,6},{6,2},{3,7},{7,3},{8,12},{12,8},{9,1... | collective-permute-start | bytes 73736 | tf_op jit(solution)/shard_map/ppermute | solution.py:46
  72.2 0.9 collective-permute-done.16.refs_5_.refs_7_.other
  73.1 1.1 backward.3
  74.2 4.8 %collective-permute-start.19 = (bf16[4,256,256]{2,1,0:T(8,128)(2,1)S(1)}, bf16[4,256,256]{2,1,0:T(8,128)(2,1)S(1)}, u32[]{:S(2)}, u32[]{:S(2)}) collective-permute-start(bf16[4,256,256]{2,1,0:T(8,128)(2,1)S(1)} %get-tuple-element.63), channel_id=1, source_target_pairs={{0,24},{8,0},{16,8},{24,16},{1,25},{9,1},{17,9},{25,17},{2,26},{10... | collective-permute-start | bytes 1572872 | tf_op jit(solution)/shard_map/ppermute | solution.py:46
  79.1 3.7 %backward.4 = (f32[128,1024]{1,0:T(8,128)S(1)}, f32[128,1024]{1,0:T(8,128)S(1)}, bf16[4,256,256]{2,1,0:T(8,128)(2,1)S(1)}, bf16[4,256,256]{2,1,0:T(8,128)(2,1)},...) custom-call(s32[33]{0:T(128)S(1)} %pad_add_fusion.info, ...), custom_call_target="tpu_custom_call" | custom-call | flops 200000000 | bytes 65536 | tf_op jit(solution)/shard_map/backward/pallas_call | solution.py:276
  82.8 0.2 collective-permute-start.21
  83.0 4.3 %collective-permute-start.22 = (bf16[4,256,256]{2,1,0:T(8,128)(2,1)S(1)}, bf16[4,256,256]{2,1,0:T(8,128)(2,1)S(1)}, u32[]{:S(2)}, u32[]{:S(2)}) collective-permute-start(bf16[4,256,256]{2,1,0:T(8,128)(2,1)S(1)} %get-tuple-element.66), channel_id=1, source_target_pairs={{0,24},{8,0},{16,8},{24,16},{1,25},{9,1},{17,9},{25,17},{2,26},{10... | collective-permute-start | bytes 1572872 | tf_op jit(solution)/shard_map/ppermute | solution.py:46
  87.4 3.6 %collective-permute-done.23 = bf16[4,256,256]{2,1,0:T(8,128)(2,1)S(1)} collective-permute-done((bf16[4,256,256]{2,1,0:T(8,128)(2,1)S(1)}, bf16[4,256,256]{2,1,0:T(8,128)(2,1)S(1)}, u32[]{:S(2)}, u32[]{:S(2)}) %collective-permute-start.23) | collective-permute-done | bytes 524320 | tf_op jit(solution)/shard_map/ppermute | solution.py:46
  91.1 0.3 collective-permute-start.24
  91.5 0.9 add_convert_fusion.1
  92.4 2.6 %collective-permute-start.20 = (bf16[4,256,256]{2,1,0:T(8,128)(2,1)}, bf16[4,256,256]{2,1,0:T(8,128)(2,1)}, u32[]{:S(2)}, u32[]{:S(2)}) collective-permute-start(bf16[4,256,256]{2,1,0:T(8,128)(2,1)} %add_convert_fusion.1), channel_id=1, source_target_pairs={{0,24},{8,0},{16,8},{24,16},{1,25},{9,1},{17,9},{25,17},{2,26},{10... | collective-permute-start | bytes 1572872 | tf_op jit(solution)/shard_map/ppermute | solution.py:46
  95.0 1.9 %collective-permute-start.17 = (f32[128,1024]{1,0:T(8,128)}, f32[128,1024]{1,0:T(8,128)S(1)}, u32[]{:S(2)}, u32[]{:S(2)}) collective-permute-start(f32[128,1024]{1,0:T(8,128)} %get-tuple-element.52), channel_id=1, source_target_pairs={{0,4},{4,0},{1,5},{5,1},{2,6},{6,2},{3,7},{7,3},{8,12},{12,8},{9,1... | collective-permute-start | bytes 1572872 | tf_op jit(solution)/shard_map/ppermute | solution.py:46
  96.9 2.7 %backward.5 = (f32[128,1024]{1,0:T(8,128)S(1)}, f32[128,1024]{1,0:T(8,128)S(1)}, bf16[4,256,256]{2,1,0:T(8,128)(2,1)S(1)}, bf16[4,256,256]{2,1,0:T(8,128)(2,1)S(1)}) custom-call(s32[33]{0:T(128)S(1)} %pad_add_fusion.info, bf16[4,256,256]{2,1,0:T(8,128)(2,1)S(1)} %copy-done.1, bf16[4,256,256]{2,1,0:T(8,128)(2,1)S(1)} %copy-done.3, ...), custom_call_target="tpu_custom_call" | custom-call | flops 200000000 | bytes 65536 | tf_op jit(solution)/shard_map/backward/pallas_call | solution.py:276
  99.7 0.8 copy-done.4
  100.5 0.8 copy-done.5
  101.3 2.0 %collective-permute-start.18 = (f32[128,1024]{1,0:T(8,128)S(1)}, f32[128,1024]{1,0:T(8,128)S(1)}, u32[]{:S(2)}, u32[]{:S(2)}) collective-permute-start(f32[128,1024]{1,0:T(8,128)S(1)} %get-tuple-element.58), channel_id=1, source_target_pairs={{0,4},{4,0},{1,5},{5,1},{2,6},{6,2},{3,7},{7,3},{8,12},{12,8},{9,1... | collective-permute-start | bytes 1572872 | tf_op jit(solution)/shard_map/ppermute | solution.py:46
  103.2 10.2 %collective-permute-done.24.three = bf16[4,256,256]{2,1,0:T(8,128)(2,1)S(1)} collective-permute-done((bf16[4,256,256]{2,1,0:T(8,128)(2,1)S(1)}, bf16[4,256,256]{2,1,0:T(8,128)(2,1)S(1)}, u32[]{:S(2)}, u32[]{:S(2)}) %collective-permute-start.24) | collective-permute-done | bytes 524320 | tf_op jit(solution)/shard_map/ppermute | solution.py:46
  113.5 0.8 copy-done.10
  114.3 2.2 %sum_high.1 = (f32[256,256]{1,0:T(8,128)}, bf16[256,256]{1,0:T(8,128)(2,1)}, bf16[256,256]{1,0:T(8,128)(2,1)}, bf16[256,256]{1,0:T(8,128)(2,1)}) custom-call(bf16[4,256,256]{2,1,0:T(8,128)(2,1)} %copy-done.5, bf16[4,256,256]{2,1,0:T(8,128)(2,1)} %copy-done.9, bf16[4,256,256]{2,1,0:T(8,128)(2,1)} %copy-done.10), custom_call_target="tpu_custom_call" | custom-call | flops 100000000 | bytes 65536 | tf_op jit(solution)/shard_map/sum_high/pallas_call | solution.py:362
  116.5 6.6 %collective-permute-start.25 = (bf16[256,256]{1,0:T(8,128)(2,1)}, bf16[256,256]{1,0:T(8,128)(2,1)S(1)}, u32[]{:S(2)}, u32[]{:S(2)}) collective-permute-start(bf16[256,256]{1,0:T(8,128)(2,1)} %get-tuple-element.70), channel_id=1, source_target_pairs={{0,224},{32,0},{64,32},{96,64},{128,96},{160,128},{192,160},{224,1... | collective-permute-start | bytes 393224 | tf_op jit(solution)/shard_map/ppermute | solution.py:46
  123.1 0.7 collective-permute-start.26
  123.8 0.6 collective-permute-start.27
  124.4 2.2 %collective-permute-done.25.down = bf16[256,256]{1,0:T(8,128)(2,1)S(1)} collective-permute-done((bf16[256,256]{1,0:T(8,128)(2,1)}, bf16[256,256]{1,0:T(8,128)(2,1)S(1)}, u32[]{:S(2)}, u32[]{:S(2)}) %collective-permute-start.25) | collective-permute-done | bytes 131104 | tf_op jit(solution)/shard_map/ppermute | solution.py:46
  126.6 4.5 %collective-permute-done.26.far = bf16[256,256]{1,0:T(8,128)(2,1)S(1)} collective-permute-done((bf16[256,256]{1,0:T(8,128)(2,1)}, bf16[256,256]{1,0:T(8,128)(2,1)S(1)}, u32[]{:S(2)}, u32[]{:S(2)}) %collective-permute-start.26) | collective-permute-done | bytes 131104 | tf_op jit(solution)/shard_map/ppermute | solution.py:46
  131.0 0.7 copy-done.14
  131.7 2.6 %sum_low.1 = (f32[256,256]{1,0:T(8,128)}, bf16[256,256]{1,0:T(8,128)(2,1)}, bf16[256,256]{1,0:T(8,128)(2,1)}, bf16[256,256]{1,0:T(8,128)(2,1)}, bf16[256,256]{1,0:T(8,128)(2,1)}) custom-call(bf16[4,256,256]{2,1,0:T(8,128)(2,1)} %copy-done.4, bf16[4,256,256]{2,1,0:T(8,128)(2,1)} %collective-permute-done.20.one, bf16[4,256,256]{2,1,0:T(8,128)(2,1)} %copy-done.8, ...), custom_call_target="tpu_custom_call" | custom-call | flops 100000000 | bytes 65536 | tf_op jit(solution)/shard_map/sum_low/pallas_call | solution.py:383
  134.3 4.4 %collective-permute-start.29 = (bf16[256,256]{1,0:T(8,128)(2,1)}, bf16[256,256]{1,0:T(8,128)(2,1)S(1)}, u32[]{:S(2)}, u32[]{:S(2)}) collective-permute-start(bf16[256,256]{1,0:T(8,128)(2,1)} %get-tuple-element.75), channel_id=1, source_target_pairs={{0,192},{32,224},{64,0},{96,32},{128,64},{160,96},{192,128},{224,1... | collective-permute-start | bytes 393224 | tf_op jit(solution)/shard_map/ppermute | solution.py:46
  138.7 1.5 collective-permute-start.31
  140.2 1.0 finish.1
  141.3 1.2 collective-permute-done.29.b
  142.5 3.3 %collective-permute-done.30.c = bf16[256,256]{1,0:T(8,128)(2,1)S(1)} collective-permute-done((bf16[256,256]{1,0:T(8,128)(2,1)}, bf16[256,256]{1,0:T(8,128)(2,1)S(1)}, u32[]{:S(2)}, u32[]{:S(2)}) %collective-permute-start.30) | collective-permute-done | bytes 131104 | tf_op jit(solution)/shard_map/ppermute | solution.py:46
  145.8 0.6 copy-done.17
  146.5 1.9 %close.1 = (bf16[256,128]{1,0:T(8,128)(2,1)}, bf16[256,128]{1,0:T(8,128)(2,1)}) custom-call(f32[256,256]{1,0:T(8,128)} %get-tuple-element.73.own, bf16[256,256]{1,0:T(8,128)(2,1)} %copy-done.15, bf16[256,256]{1,0:T(8,128)(2,1)} %copy-done.16, bf16[256,256]{1,0:T(8,128)(2,1)} %copy-done.17, bf16[256,256]{1,0:T(8,128)(2,1)} %copy-done.18), custom_call_target="tpu_custom_call" | custom-call | tf_op jit(solution)/shard_map/close/pallas_call | solution.py:399
  (81 shorter events, 1.0 us)
Async XLA Ops:
  2.2 10.4 %collective-permute-start.8 = (bf16[256,256]{1,0:T(8,128)(2,1)}, bf16[256,256]{1,0:T(8,128)(2,1)S(1)}, u32[]{:S(2)}, u32[]{:S(2)}) collective-permute-start(bf16[256,256]{1,0:T(8,128)(2,1)} %join.1.refs_0_), channel_id=1, source_target_pairs={{0,192},{32,224},{64,0},{96,32},{128,64},{160,96},{192,128},{224,1... | collective-permute-start | bytes 393224 | tf_op jit(solution)/shard_map/ppermute | solution.py:46
  9.0 8.3 %collective-permute-start = (bf16[256,256]{1,0:T(8,128)(2,1)}, bf16[256,256]{1,0:T(8,128)(2,1)S(1)}, u32[]{:S(2)}, u32[]{:S(2)}) collective-permute-start(bf16[256,256]{1,0:T(8,128)(2,1)} %join.1.refs_0_), channel_id=1, source_target_pairs={{0,64},{32,96},{64,128},{96,160},{128,192},{160,224},{192,0},{224,... | collective-permute-start | bytes 393224 | tf_op jit(solution)/shard_map/ppermute | solution.py:46
  9.0 9.7 %collective-permute-start.5 = (bf16[256,256]{1,0:T(8,128)(2,1)}, bf16[256,256]{1,0:T(8,128)(2,1)S(1)}, u32[]{:S(2)}, u32[]{:S(2)}) collective-permute-start(bf16[256,256]{1,0:T(8,128)(2,1)} %join.1.refs_0_), channel_id=1, source_target_pairs={{0,224},{32,0},{64,32},{96,64},{128,96},{160,128},{192,160},{224,1... | collective-permute-start | bytes 393224 | tf_op jit(solution)/shard_map/ppermute | solution.py:46
  12.2 9.2 %collective-permute-start.4 = (bf16[256,256]{1,0:T(8,128)(2,1)}, bf16[256,256]{1,0:T(8,128)(2,1)S(1)}, u32[]{:S(2)}, u32[]{:S(2)}) collective-permute-start(bf16[256,256]{1,0:T(8,128)(2,1)} %join.1.refs_0_), channel_id=1, source_target_pairs={{0,32},{32,64},{64,96},{96,128},{128,160},{160,192},{192,224},{224... | collective-permute-start | bytes 393224 | tf_op jit(solution)/shard_map/ppermute | solution.py:46
  12.6 11.4 %copy-start.19 = (bf16[256,256]{1,0:T(8,128)(2,1)}, bf16[256,256]{1,0:T(8,128)(2,1)S(1)}, u32[]{:S(2)}) copy-start(bf16[256,256]{1,0:T(8,128)(2,1)S(1)} %collective-permute-done.8.refs_0_) | copy-start | bytes 393220
  12.6 12.6 %collective-permute-start.9 = (bf16[256,256]{1,0:T(8,128)(2,1)S(1)}, bf16[256,256]{1,0:T(8,128)(2,1)S(1)}, u32[]{:S(2)}, u32[]{:S(2)}) collective-permute-start(bf16[256,256]{1,0:T(8,128)(2,1)S(1)} %collective-permute-done.8.refs_0_), channel_id=1, source_target_pairs={{0,224},{32,0},{64,32},{96,64},{128,96},{160,128},{192,160},{224,1... | collective-permute-start | bytes 393224 | tf_op jit(solution)/shard_map/ppermute | solution.py:46
  17.4 4.0 %copy-start.20 = (bf16[256,256]{1,0:T(8,128)(2,1)}, bf16[256,256]{1,0:T(8,128)(2,1)S(1)}, u32[]{:S(2)}) copy-start(bf16[256,256]{1,0:T(8,128)(2,1)S(1)} %collective-permute-done.refs_3_) | copy-start | bytes 393220
  17.4 7.8 %collective-permute-start.10 = (bf16[256,256]{1,0:T(8,128)(2,1)S(1)}, bf16[256,256]{1,0:T(8,128)(2,1)S(1)}, u32[]{:S(2)}, u32[]{:S(2)}) collective-permute-start(bf16[256,256]{1,0:T(8,128)(2,1)S(1)} %collective-permute-done.refs_3_), channel_id=1, source_target_pairs={{0,64},{32,96},{64,128},{96,160},{128,192},{160,224},{192,0},{224,... | collective-permute-start | bytes 393224 | tf_op jit(solution)/shard_map/ppermute | solution.py:46
  17.4 11.6 %collective-permute-start.1 = (bf16[256,256]{1,0:T(8,128)(2,1)S(1)}, bf16[256,256]{1,0:T(8,128)(2,1)S(1)}, u32[]{:S(2)}, u32[]{:S(2)}) collective-permute-start(bf16[256,256]{1,0:T(8,128)(2,1)S(1)} %collective-permute-done.refs_3_), channel_id=1, source_target_pairs={{0,32},{32,64},{64,96},{96,128},{128,160},{160,192},{192,224},{224... | collective-permute-start | bytes 393224 | tf_op jit(solution)/shard_map/ppermute | solution.py:46
  18.8 2.6 %copy-start.23 = (bf16[256,256]{1,0:T(8,128)(2,1)}, bf16[256,256]{1,0:T(8,128)(2,1)S(1)}, u32[]{:S(2)}) copy-start(bf16[256,256]{1,0:T(8,128)(2,1)S(1)} %collective-permute-done.5.refs_2_) | copy-start | bytes 393220
  21.4 0.7 copy-start.24
  24.0 10.1 %copy-start.25 = (s32[1,32,32]{2,1,0:T(8,128)S(1)}, s32[1,32,32]{2,1,0:T(8,128)}, u32[]{:S(2)}) copy-start(s32[1,32,32]{2,1,0:T(8,128)} %param.9) | copy-start | bytes 12292
  24.0 24.3 %collective-permute-start.6 = (bf16[4,256,256]{2,1,0:T(8,128)(2,1)}, bf16[4,256,256]{2,1,0:T(8,128)(2,1)S(1)}, u32[]{:S(2)}, u32[]{:S(2)}) collective-permute-start(bf16[4,256,256]{2,1,0:T(8,128)(2,1)} %stack.2.refs_0_), channel_id=1, source_target_pairs={{0,8},{8,16},{16,24},{24,0},{1,9},{9,17},{17,25},{25,1},{2,10},{10... | collective-permute-start | bytes 1572872 | tf_op jit(solution)/shard_map/ppermute | solution.py:46
  25.2 3.8 %copy-start.21 = (bf16[256,256]{1,0:T(8,128)(2,1)}, bf16[256,256]{1,0:T(8,128)(2,1)S(1)}, u32[]{:S(2)}) copy-start(bf16[256,256]{1,0:T(8,128)(2,1)S(1)} %collective-permute-done.9.refs_2_) | copy-start | bytes 393220
  25.2 3.8 %copy-start.22 = (bf16[256,256]{1,0:T(8,128)(2,1)}, bf16[256,256]{1,0:T(8,128)(2,1)S(1)}, u32[]{:S(2)}) copy-start(bf16[256,256]{1,0:T(8,128)(2,1)S(1)} %collective-permute-done.10.refs_3_) | copy-start | bytes 393220
  29.0 0.7 copy-start.11
  31.6 11.0 %copy-start.1 = (bf16[4,256,256]{2,1,0:T(8,128)(2,1)S(1)}, bf16[4,256,256]{2,1,0:T(8,128)(2,1)}, u32[]{:S(2)}) copy-start(bf16[4,256,256]{2,1,0:T(8,128)(2,1)} %stack.2.refs_0_) | copy-start | bytes 1572868
  31.6 16.8 %collective-permute-start.11 = (bf16[4,256,256]{2,1,0:T(8,128)(2,1)}, bf16[4,256,256]{2,1,0:T(8,128)(2,1)S(1)}, u32[]{:S(2)}, u32[]{:S(2)}) collective-permute-start(bf16[4,256,256]{2,1,0:T(8,128)(2,1)} %stack.3.refs_1_), channel_id=1, source_target_pairs={{0,24},{8,0},{16,8},{24,16},{1,25},{9,1},{17,9},{25,17},{2,26},{10... | collective-permute-start | bytes 1572872 | tf_op jit(solution)/shard_map/ppermute | solution.py:46
  36.7 3.0 %collective-permute-start.2 = (s32[8,128]{1,0:T(8,128)}, s32[8,128]{1,0:T(8,128)S(1)}, u32[]{:S(2)}, u32[]{:S(2)}) collective-permute-start(s32[8,128]{1,0:T(8,128)} %get-tuple-element.42), channel_id=1, source_target_pairs={{0,1},{1,0},{2,3},{3,2},{4,5},{5,4},{6,7},{7,6},{8,9},{9,8},{10,11... | collective-permute-start | bytes 12296 | tf_op jit(solution)/shard_map/ppermute | solution.py:406
  38.0 1.7 %copy-start.26 = (s32[8,128]{1,0:T(8,128)S(1)}, s32[8,128]{1,0:T(8,128)}, u32[]{:S(2)}) copy-start(s32[8,128]{1,0:T(8,128)} %get-tuple-element.42) | copy-start | bytes 12292
  39.6 4.5 %collective-permute-start.3 = (s32[8,128]{1,0:T(8,128)S(1)}, s32[8,128]{1,0:T(8,128)S(1)}, u32[]{:S(2)}, u32[]{:S(2)}) collective-permute-start(s32[8,128]{1,0:T(8,128)S(1)} %add.110), channel_id=1, source_target_pairs={{0,2},{2,0},{1,3},{3,1},{4,6},{6,4},{5,7},{7,5},{8,10},{10,8},{9,1... | collective-permute-start | bytes 12296 | tf_op jit(solution)/shard_map/ppermute | solution.py:407
  42.6 12.8 %collective-permute-start.14 = (bf16[4,256,256]{2,1,0:T(8,128)(2,1)S(1)}, bf16[4,256,256]{2,1,0:T(8,128)(2,1)S(1)}, u32[]{:S(2)}, u32[]{:S(2)}) collective-permute-start(bf16[4,256,256]{2,1,0:T(8,128)(2,1)S(1)} %copy-done.1), channel_id=1, source_target_pairs={{0,24},{8,0},{16,8},{24,16},{1,25},{9,1},{17,9},{25,17},{2,26},{10... | collective-permute-start | bytes 1572872 | tf_op jit(solution)/shard_map/ppermute | solution.py:46
  43.2 12.2 %collective-permute-start.15 = (bf16[4,256,256]{2,1,0:T(8,128)(2,1)}, bf16[4,256,256]{2,1,0:T(8,128)(2,1)S(1)}, u32[]{:S(2)}, u32[]{:S(2)}) collective-permute-start(bf16[4,256,256]{2,1,0:T(8,128)(2,1)} %stack.3.refs_1_), channel_id=1, source_target_pairs={{0,8},{8,16},{16,24},{24,0},{1,9},{9,17},{17,25},{25,1},{2,10},{10... | collective-permute-start | bytes 1572872 | tf_op jit(solution)/shard_map/ppermute | solution.py:46
  44.1 7.3 %collective-permute-start.13 = (bf16[2,1024,128]{2,1,0:T(8,128)(2,1)}, bf16[2,1024,128]{2,1,0:T(8,128)(2,1)S(1)}, u32[]{:S(2)}, u32[]{:S(2)}) collective-permute-start(bf16[2,1024,128]{2,1,0:T(8,128)(2,1)} %get-tuple-element.43.refs_2_.refs_4_), channel_id=1, source_target_pairs={{0,4},{4,0},{1,5},{5,1},{2,6},{6,2},{3,7},{7,3},{8,12},{12,8},{9,1... | collective-permute-start | bytes 1572872 | tf_op jit(solution)/shard_map/ppermute | solution.py:46
  48.2 17.3 %collective-permute-start.7 = (bf16[4,256,256]{2,1,0:T(8,128)(2,1)S(1)}, bf16[4,256,256]{2,1,0:T(8,128)(2,1)S(1)}, u32[]{:S(2)}, u32[]{:S(2)}) collective-permute-start(bf16[4,256,256]{2,1,0:T(8,128)(2,1)S(1)} %collective-permute-done.6.refs_0_), channel_id=1, source_target_pairs={{0,8},{8,16},{16,24},{24,0},{1,9},{9,17},{17,25},{25,1},{2,10},{10... | collective-permute-start | bytes 1572872 | tf_op jit(solution)/shard_map/ppermute | solution.py:46
  48.3 17.9 %collective-permute-start.12 = (bf16[4,256,256]{2,1,0:T(8,128)(2,1)S(1)}, bf16[4,256,256]{2,1,0:T(8,128)(2,1)S(1)}, u32[]{:S(2)}, u32[]{:S(2)}) collective-permute-start(bf16[4,256,256]{2,1,0:T(8,128)(2,1)S(1)} %collective-permute-done.11.refs_3_), channel_id=1, source_target_pairs={{0,24},{8,0},{16,8},{24,16},{1,25},{9,1},{17,9},{25,17},{2,26},{10... | collective-permute-start | bytes 1572872 | tf_op jit(solution)/shard_map/ppermute | solution.py:46
  51.4 1.1 copy-start
  52.4 1.0 copy-start.2
  68.2 5.9 %copy-start.6 = (f32[128,1024]{1,0:T(8,128)}, f32[128,1024]{1,0:T(8,128)S(1)}, u32[]{:S(2)}) copy-start(f32[128,1024]{1,0:T(8,128)S(1)} %get-tuple-element.51.acc_mine) | copy-start | bytes 1572868
  68.2 4.8 %collective-permute-start.16 = (f32[2,3,1024]{2,1,0:T(4,128)S(1)}, f32[2,3,1024]{2,1,0:T(4,128)S(1)}, u32[]{:S(2)}, u32[]{:S(2)}) collective-permute-start(f32[2,3,1024]{2,1,0:T(4,128)S(1)} %get-tuple-element.50.refs_4_.refs_6_.mine), channel_id=1, source_target_pairs={{0,4},{4,0},{1,5},{5,1},{2,6},{6,2},{3,7},{7,3},{8,12},{12,8},{9,1... | collective-permute-start | bytes 73736 | tf_op jit(solution)/shard_map/ppermute | solution.py:46
  74.1 16.9 %collective-permute-start.23 = (bf16[4,256,256]{2,1,0:T(8,128)(2,1)S(1)}, bf16[4,256,256]{2,1,0:T(8,128)(2,1)S(1)}, u32[]{:S(2)}, u32[]{:S(2)}) collective-permute-start(bf16[4,256,256]{2,1,0:T(8,128)(2,1)S(1)} %get-tuple-element.68), channel_id=1, source_target_pairs={{0,8},{8,16},{16,24},{24,0},{1,9},{9,17},{17,25},{25,1},{2,10},{10... | collective-permute-start | bytes 1572872 | tf_op jit(solution)/shard_map/ppermute | solution.py:46
  74.2 17.2 %collective-permute-start.19 = (bf16[4,256,256]{2,1,0:T(8,128)(2,1)S(1)}, bf16[4,256,256]{2,1,0:T(8,128)(2,1)S(1)}, u32[]{:S(2)}, u32[]{:S(2)}) collective-permute-start(bf16[4,256,256]{2,1,0:T(8,128)(2,1)S(1)} %get-tuple-element.63), channel_id=1, source_target_pairs={{0,24},{8,0},{16,8},{24,16},{1,25},{9,1},{17,9},{25,17},{2,26},{10... | collective-permute-start | bytes 1572872 | tf_op jit(solution)/shard_map/ppermute | solution.py:46
  82.8 40.3 %collective-permute-start.21 = (bf16[4,256,256]{2,1,0:T(8,128)(2,1)}, bf16[4,256,256]{2,1,0:T(8,128)(2,1)S(1)}, u32[]{:S(2)}, u32[]{:S(2)}) collective-permute-start(bf16[4,256,256]{2,1,0:T(8,128)(2,1)} %get-tuple-element.64), channel_id=1, source_target_pairs={{0,8},{8,16},{16,24},{24,0},{1,9},{9,17},{17,25},{25,1},{2,10},{10... | collective-permute-start | bytes 1572872 | tf_op jit(solution)/shard_map/ppermute | solution.py:46
  83.0 18.2 %collective-permute-start.22 = (bf16[4,256,256]{2,1,0:T(8,128)(2,1)S(1)}, bf16[4,256,256]{2,1,0:T(8,128)(2,1)S(1)}, u32[]{:S(2)}, u32[]{:S(2)}) collective-permute-start(bf16[4,256,256]{2,1,0:T(8,128)(2,1)S(1)} %get-tuple-element.66), channel_id=1, source_target_pairs={{0,24},{8,0},{16,8},{24,16},{1,25},{9,1},{17,9},{25,17},{2,26},{10... | collective-permute-start | bytes 1572872 | tf_op jit(solution)/shard_map/ppermute | solution.py:46
  91.1 22.3 %collective-permute-start.24 = (bf16[4,256,256]{2,1,0:T(8,128)(2,1)S(1)}, bf16[4,256,256]{2,1,0:T(8,128)(2,1)S(1)}, u32[]{:S(2)}, u32[]{:S(2)}) collective-permute-start(bf16[4,256,256]{2,1,0:T(8,128)(2,1)S(1)} %add_convert_fusion), channel_id=1, source_target_pairs={{0,8},{8,16},{16,24},{24,0},{1,9},{9,17},{17,25},{25,1},{2,10},{10... | collective-permute-start | bytes 1572872 | tf_op jit(solution)/shard_map/ppermute | solution.py:46
  91.5 5.5 %copy-start.3 = (bf16[4,256,256]{2,1,0:T(8,128)(2,1)S(1)}, bf16[4,256,256]{2,1,0:T(8,128)(2,1)}, u32[]{:S(2)}) copy-start(bf16[4,256,256]{2,1,0:T(8,128)(2,1)} %stack.3.refs_1_) | copy-start | bytes 1572868
  92.4 31.4 %collective-permute-start.20 = (bf16[4,256,256]{2,1,0:T(8,128)(2,1)}, bf16[4,256,256]{2,1,0:T(8,128)(2,1)}, u32[]{:S(2)}, u32[]{:S(2)}) collective-permute-start(bf16[4,256,256]{2,1,0:T(8,128)(2,1)} %add_convert_fusion.1), channel_id=1, source_target_pairs={{0,24},{8,0},{16,8},{24,16},{1,25},{9,1},{17,9},{25,17},{2,26},{10... | collective-permute-start | bytes 1572872 | tf_op jit(solution)/shard_map/ppermute | solution.py:46
  95.0 43.7 %collective-permute-start.17 = (f32[128,1024]{1,0:T(8,128)}, f32[128,1024]{1,0:T(8,128)S(1)}, u32[]{:S(2)}, u32[]{:S(2)}) collective-permute-start(f32[128,1024]{1,0:T(8,128)} %get-tuple-element.52), channel_id=1, source_target_pairs={{0,4},{4,0},{1,5},{5,1},{2,6},{6,2},{3,7},{7,3},{8,12},{12,8},{9,1... | collective-permute-start | bytes 1572872 | tf_op jit(solution)/shard_map/ppermute | solution.py:46
  99.7 0.8 copy-start.4
  100.5 0.8 copy-start.5
  101.3 2.0 %copy-start.9 = (bf16[4,256,256]{2,1,0:T(8,128)(2,1)}, bf16[4,256,256]{2,1,0:T(8,128)(2,1)S(1)}, u32[]{:S(2)}) copy-start(bf16[4,256,256]{2,1,0:T(8,128)(2,1)S(1)} %collective-permute-done.22.one) | copy-start | bytes 1572868
  101.3 38.9 %collective-permute-start.18 = (f32[128,1024]{1,0:T(8,128)S(1)}, f32[128,1024]{1,0:T(8,128)S(1)}, u32[]{:S(2)}, u32[]{:S(2)}) collective-permute-start(f32[128,1024]{1,0:T(8,128)S(1)} %get-tuple-element.58), channel_id=1, source_target_pairs={{0,4},{4,0},{1,5},{5,1},{2,6},{6,2},{3,7},{7,3},{8,12},{12,8},{9,1... | collective-permute-start | bytes 1572872 | tf_op jit(solution)/shard_map/ppermute | solution.py:46
  113.5 0.8 copy-start.10
  116.5 10.1 %collective-permute-start.25 = (bf16[256,256]{1,0:T(8,128)(2,1)}, bf16[256,256]{1,0:T(8,128)(2,1)S(1)}, u32[]{:S(2)}, u32[]{:S(2)}) collective-permute-start(bf16[256,256]{1,0:T(8,128)(2,1)} %get-tuple-element.70), channel_id=1, source_target_pairs={{0,224},{32,0},{64,32},{96,64},{128,96},{160,128},{192,160},{224,1... | collective-permute-start | bytes 393224 | tf_op jit(solution)/shard_map/ppermute | solution.py:46
  123.1 8.6 %copy-start.8 = (bf16[4,256,256]{2,1,0:T(8,128)(2,1)}, bf16[4,256,256]{2,1,0:T(8,128)(2,1)S(1)}, u32[]{:S(2)}) copy-start(bf16[4,256,256]{2,1,0:T(8,128)(2,1)S(1)} %collective-permute-done.21.three) | copy-start | bytes 1572868
  123.1 7.9 %collective-permute-start.26 = (bf16[256,256]{1,0:T(8,128)(2,1)}, bf16[256,256]{1,0:T(8,128)(2,1)S(1)}, u32[]{:S(2)}, u32[]{:S(2)}) collective-permute-start(bf16[256,256]{1,0:T(8,128)(2,1)} %get-tuple-element.71), channel_id=1, source_target_pairs={{0,192},{32,224},{64,0},{96,32},{128,64},{160,96},{192,128},{224,1... | collective-permute-start | bytes 393224 | tf_op jit(solution)/shard_map/ppermute | solution.py:46
  123.8 7.3 %collective-permute-start.27 = (bf16[256,256]{1,0:T(8,128)(2,1)}, bf16[256,256]{1,0:T(8,128)(2,1)S(1)}, u32[]{:S(2)}, u32[]{:S(2)}) collective-permute-start(bf16[256,256]{1,0:T(8,128)(2,1)} %get-tuple-element.72), channel_id=1, source_target_pairs={{0,32},{32,64},{64,96},{96,128},{128,160},{160,192},{192,224},{224... | collective-permute-start | bytes 393224 | tf_op jit(solution)/shard_map/ppermute | solution.py:46
  126.6 5.2 %copy-start.12 = (bf16[256,256]{1,0:T(8,128)(2,1)}, bf16[256,256]{1,0:T(8,128)(2,1)S(1)}, u32[]{:S(2)}) copy-start(bf16[256,256]{1,0:T(8,128)(2,1)S(1)} %collective-permute-done.25.down) | copy-start | bytes 393220
  131.0 0.7 copy-start.13
  131.0 0.7 copy-start.14
  131.7 8.4 %copy-start.7 = (f32[128,1024]{1,0:T(8,128)S(1)}, f32[128,1024]{1,0:T(8,128)}, u32[]{:S(2)}) copy-start(f32[128,1024]{1,0:T(8,128)} %copy-done.6) | copy-start | bytes 1572868
  134.3 7.0 %collective-permute-start.28 = (bf16[256,256]{1,0:T(8,128)(2,1)}, bf16[256,256]{1,0:T(8,128)(2,1)S(1)}, u32[]{:S(2)}, u32[]{:S(2)}) collective-permute-start(bf16[256,256]{1,0:T(8,128)(2,1)} %get-tuple-element.74), channel_id=1, source_target_pairs={{0,64},{32,96},{64,128},{96,160},{128,192},{160,224},{192,0},{224,... | collective-permute-start | bytes 393224 | tf_op jit(solution)/shard_map/ppermute | solution.py:46
  134.3 8.2 %collective-permute-start.29 = (bf16[256,256]{1,0:T(8,128)(2,1)}, bf16[256,256]{1,0:T(8,128)(2,1)S(1)}, u32[]{:S(2)}, u32[]{:S(2)}) collective-permute-start(bf16[256,256]{1,0:T(8,128)(2,1)} %get-tuple-element.75), channel_id=1, source_target_pairs={{0,192},{32,224},{64,0},{96,32},{128,64},{160,96},{192,128},{224,1... | collective-permute-start | bytes 393224 | tf_op jit(solution)/shard_map/ppermute | solution.py:46
  138.7 7.1 %collective-permute-start.30 = (bf16[256,256]{1,0:T(8,128)(2,1)}, bf16[256,256]{1,0:T(8,128)(2,1)S(1)}, u32[]{:S(2)}, u32[]{:S(2)}) collective-permute-start(bf16[256,256]{1,0:T(8,128)(2,1)} %get-tuple-element.76), channel_id=1, source_target_pairs={{0,224},{32,0},{64,32},{96,64},{128,96},{160,128},{192,160},{224,1... | collective-permute-start | bytes 393224 | tf_op jit(solution)/shard_map/ppermute | solution.py:46
  138.7 7.1 %collective-permute-start.31 = (bf16[256,256]{1,0:T(8,128)(2,1)}, bf16[256,256]{1,0:T(8,128)(2,1)S(1)}, u32[]{:S(2)}, u32[]{:S(2)}) collective-permute-start(bf16[256,256]{1,0:T(8,128)(2,1)} %get-tuple-element.77), channel_id=1, source_target_pairs={{0,32},{32,64},{64,96},{96,128},{128,160},{160,192},{192,224},{224... | collective-permute-start | bytes 393224 | tf_op jit(solution)/shard_map/ppermute | solution.py:46
  141.3 4.5 %copy-start.15 = (bf16[256,256]{1,0:T(8,128)(2,1)}, bf16[256,256]{1,0:T(8,128)(2,1)S(1)}, u32[]{:S(2)}) copy-start(bf16[256,256]{1,0:T(8,128)(2,1)S(1)} %collective-permute-done.28.a) | copy-start | bytes 393220
  142.5 3.3 %copy-start.16 = (bf16[256,256]{1,0:T(8,128)(2,1)}, bf16[256,256]{1,0:T(8,128)(2,1)S(1)}, u32[]{:S(2)}) copy-start(bf16[256,256]{1,0:T(8,128)(2,1)S(1)} %collective-permute-done.29.b) | copy-start | bytes 393220
  145.8 0.7 copy-start.17
  145.8 0.7 copy-start.18
